TPU v7x, 32 devices: a whole 2x2x4 slice. The times are simulated.
32 devices in a mesh: dp: 16 (over z, x, core), tensor: 2 (over y).
Axes of the slice: x: 2, y: 2, z: 4, core: 2. Of those that a mesh axis runs over, the one named last changes fastest.
Arguments:
- stream: bfloat16 [9216, 767], P('dp'), may hold values from -6 to 6
- w_query: bfloat16 [768, 768], P('dp', 'tensor'), may hold values from -0.21875 to 0.21875
- w_key: bfloat16 [768, 768], P('dp', 'tensor'), may hold values from -0.21875 to 0.21875
- w_value: bfloat16 [768, 768], P('dp', 'tensor'), may hold values from -0.21875 to 0.21875
- b_query: bfloat16 [768], P('tensor'), may hold values from -4 to 4
- b_value: bfloat16 [768], P('tensor'), may hold values from -4 to 4
- w_out: bfloat16 [768, 768], P('tensor', 'dp'), may hold values from -1.75 to 1.75
- b_out: bfloat16 [768], replicated, may hold values from -4 to 4
- gain_attn: bfloat16 [768], replicated, may hold values from 0.099609375 to 1.8984375
- w_up: bfloat16 [768, 3072], P('dp', 'tensor'), may hold values from -0.21875 to 0.21875
- b_up: bfloat16 [3072], P('tensor'), may hold values from -4 to 4
- w_down: bfloat16 [3072, 768], P('tensor', 'dp'), may hold values from -0.109375 to 0.109375
- b_down: bfloat16 [768], replicated, may hold values from -4 to 4
- gain_mlp: bfloat16 [768], replicated, may hold values from 0.099609375 to 1.8984375
- cotangent: bfloat16 [9216, 767], P('dp'), may hold values from -6 to 6
- lengths: int32 [16, 4], P('dp'), may hold values from 1 to 512, 576 in all within a row
Outputs:
- out: bfloat16 [9216, 767], P('dp')
- grad_stream: bfloat16 [9216, 767], P('dp')
- grad_w_query: float32 [768, 768], P('dp', 'tensor')
- grad_w_key: float32 [768, 768], P('dp', 'tensor')
- grad_w_value: float32 [768, 768], P('dp', 'tensor')
- grad_b_query: float32 [768], P('tensor')
- grad_b_value: float32 [768], P('tensor')
- grad_w_out: float32 [768, 768], P('tensor', 'dp')
- grad_b_out: float32 [768], replicated
- grad_gain_attn: float32 [768], replicated
- grad_w_up: float32 [768, 3072], P('dp', 'tensor')
- grad_b_up: float32 [3072], P('tensor')
- grad_w_down: float32 [3072, 768], P('tensor', 'dp')
- grad_b_down: float32 [768], replicated
- grad_gain_mlp: float32 [768], replicated
Inputs may be any that keep to these rules, and one draw needn't show every extreme that they name: In each row the lengths sum to 576 and one of them is exactly 512.
All inputs are finite; a program needn't handle non-finite values.
Results may differ from a plain program's by a relative error of at most 0.01.
Values may be sent and summed in bfloat16 or wider, within the bound.
No kernel may reach another device: no remote copies, remote signals or barrier semaphores. Data moves between devices by JAX's collectives and lax.ppermute only.
A program may use at most 128 MiB of HBM per device.

v0:
```python
import functools

import jax
import jax.numpy as jnp
from jax import lax
from jax.experimental import pallas as pl
from jax.experimental.pallas import tpu as pltpu
from jax.sharding import PartitionSpec as P

HD = 64
PAIR = 2 * HD
STEP = 384
epsilon = 1e-05
ROOM = 10 * 1024 * 1024
LONG = 100_000_000_000
F32 = jnp.float32
BF16 = jnp.bfloat16
VMEM = pl.BlockSpec(memory_space=pltpu.VMEM)
SMEM = pl.BlockSpec(memory_space=pltpu.SMEM)
FAR = pl.BlockSpec(memory_space=pltpu.HBM)


def phases_of(count):
    found, stride = [], 1
    while stride < count:
        rest = count // stride
        radix = 2 if stride == 1 or (rest.bit_length() - 1) % 2 == 1 else 4
        found.append((stride, radix))
        stride *= radix
    return found


def relative_order(count):
    blocks = [0]
    for stride, radix in reversed(phases_of(count)):
        blocks = [b ^ (k * stride) for k in range(radix) for b in blocks]
    return blocks


def swap(array, flip):
    count = lax.axis_size("dp")
    return lax.ppermute(array, "dp", [(i, i ^ flip) for i in range(count)])


def swap_tensor(array):
    count = lax.axis_size("tensor")
    return lax.ppermute(array, "tensor", [(i, i ^ 1) for i in range(count)])


def dot_nn(left, right):
    return lax.dot_general(left, right, (((1,), (0,)), ((), ())), preferred_element_type=F32)


def dot_nt(left, right):
    return lax.dot_general(left, right, (((1,), (1,)), ((), ())), preferred_element_type=F32)


def dot_tn(left, right):
    return lax.dot_general(left, right, (((0,), (0,)), ((), ())), preferred_element_type=F32)


def shape(rows, columns, dtype):
    return jax.ShapeDtypeStruct((rows, columns), dtype)


def after(array, *others):
    return lax.optimization_barrier((array,) + others)[0]


def call(kernel, outs, args, scalars=0, scratch=(), room=ROOM, cost=0):
    return pl.pallas_call(
        kernel,
        out_shape=outs,
        in_specs=[SMEM] * scalars + [VMEM] * (len(args) - scalars),
        out_specs=[VMEM] * len(outs),
        scratch_shapes=list(scratch),
        compiler_params=pltpu.CompilerParams(vmem_limit_bytes=room),
        cost_estimate=pl.CostEstimate(flops=cost, bytes_accessed=1024, transcendentals=0),
    )(*args)


def chooser_of(order_ref, rows):
    place = lax.broadcasted_iota(jnp.int32, (rows, order_ref.shape[1]), 0)
    return (place == order_ref[...]).astype(F32).astype(BF16)


def last_of(order_ref):
    return (order_ref[...] == order_ref.shape[1] - 1).astype(F32)


def expand(rows, last):
    return rows - jnp.sum(rows, axis=1, keepdims=True) * last


def norm_of(full):
    inverse = lax.rsqrt(jnp.mean(full * full, axis=1, keepdims=True) + epsilon)
    return full * inverse, inverse


def norm_backward(grad, normed, inverse, gain, last):
    scaled = grad * gain
    full = inverse * (scaled - normed * jnp.mean(scaled * normed, axis=1, keepdims=True))
    return (full - jnp.sum(full * last, axis=1, keepdims=True)) * (1.0 - last)


def center(rows):
    return rows - jnp.mean(rows, axis=1, keepdims=True)


def by_rows(rows, body, carry=0):
    step = next(size for size in (192, 144, 96, 48, rows) if rows % size == 0)
    return lax.fori_loop(0, rows // step, lambda i, c: body(pl.ds(pl.multiple_of(i * step, step), step), c), carry)


def pack_kernel(*refs):
    at = 0
    for ref in refs[:-1]:
        refs[-1][:, at : at + ref.shape[1]] = ref[...]
        at += ref.shape[1]


def move(sems, *pairs):
    copies = [pltpu.make_async_copy(source, target, sems.at[i]) for i, (source, target) in enumerate(pairs)]
    for copy in copies:
        copy.start()
    return copies


def pack_far_kernel(*refs):
    *parts, out_ref, sems = refs
    pairs, at = [], 0
    for ref in parts:
        pairs.append((ref, out_ref.at[:, at : at + ref.shape[1]]))
        at += ref.shape[1]
    for copy in move(sems, *pairs):
        copy.wait()


def pack(arrays, room=ROOM):
    rows, columns = arrays[0].shape[0], sum(a.shape[1] for a in arrays)
    if rows % 16:
        return call(pack_kernel, [shape(rows, columns, BF16)], arrays)[0]
    return pl.pallas_call(
        pack_far_kernel,
        out_shape=shape(rows, columns, BF16),
        in_specs=[FAR] * len(arrays),
        out_specs=VMEM,
        scratch_shapes=[pltpu.SemaphoreType.DMA((len(arrays),))],
        compiler_params=pltpu.CompilerParams(vmem_limit_bytes=room),
        cost_estimate=pl.CostEstimate(flops=0, bytes_accessed=1024, transcendentals=0),
    )(*arrays)


def joined(refs, columns=slice(None)):
    return refs[0][:, columns] if len(refs) == 1 else jnp.concatenate([ref[:, columns] for ref in refs], axis=0)


def stacked(refs, plan, columns):
    parts = [refs[i][a : a + n, columns] for i, a, n in plan]
    return parts[0] if len(parts) == 1 else jnp.concatenate(parts, axis=0)


def first_kernel(order_ref, stream_ref, gain_ref, ent_ref, acts_ref, chooser_ref):
    chooser_ref[...] = chooser_of(order_ref, order_ref.shape[1])
    last = last_of(order_ref)
    gain = gain_ref[...].astype(F32).reshape(1, -1)
    gain = dot_nn(jnp.concatenate([gain] * 8, axis=0).astype(BF16), chooser_ref[...])[0:1]
    inner = stream_ref.shape[1]

    def one(at, carry):
        entering = dot_nn(stream_ref[at, :], chooser_ref[:inner, :])
        ent_ref[at, :] = entering.astype(BF16)
        normed, _ = norm_of(expand(entering, last))
        acts_ref[at, :] = (normed * gain).astype(BF16)
        return carry

    by_rows(stream_ref.shape[0], one)


def prepare_kernel(rank_ref, order_ref, cot_ref, own_ref, other_ref, ent_in, *refs):
    vec_refs, (ctx_ref, ent_ref, top_ref, gbm_ref, row_ref) = refs[:-5], refs[-5:]
    zero = rank_ref[0, 0] == 0
    width = own_ref.shape[1]
    own, other = own_ref[...], other_ref[...]
    ctx_ref[:, :width] = jnp.where(zero, own, other)
    ctx_ref[:, width:] = jnp.where(zero, other, own)
    ent_ref[...] = ent_in[...]
    chooser = chooser_of(order_ref, order_ref.shape[1])
    plain = [ref[...].astype(F32).reshape(1, -1) for ref in vec_refs]
    rows = dot_nn(jnp.concatenate(plain + plain, axis=0).astype(BF16), chooser)
    top = dot_nn(cot_ref[...], chooser[: cot_ref.shape[1]])
    top_ref[...] = top.astype(BF16)
    gbm = center(top)
    gbm_ref[...] = gbm.astype(BF16)
    row_ref[:4, :] = rows[:4]
    row_ref[4:5, :] = jnp.sum(gbm, axis=0, keepdims=True)
    row_ref[5:, :] = jnp.zeros((row_ref.shape[0] - 5, row_ref.shape[1]), F32)


def row_blocks(rows):
    return [(i, min(rows, i + STEP)) for i in range(0, rows, STEP)]


def write_mask(len_ref, mask_ref):
    for lo, hi in row_blocks(mask_ref.shape[0]):
        place = lax.broadcasted_iota(jnp.int32, (1, hi - lo), 1) + lo
        first = jnp.zeros_like(place)
        end = jnp.int32(0)
        for j in range(len_ref.shape[1] - 1):
            end = end + len_ref[0, j]
            first = jnp.where(place >= end, end, first)
        key = lax.broadcasted_iota(jnp.int32, (hi, hi - lo), 0)
        mask_ref[:hi, lo:hi] = jnp.where((key >= first) & (key <= place), 0.0, -1e30)


def both_heads(block):
    zero = jnp.zeros_like(block)
    first = lax.broadcasted_iota(jnp.int32, block.shape, 1) < HD
    return jnp.concatenate([jnp.where(first, block, zero), jnp.where(first, zero, block)], axis=0)


def own_rows(both):
    size = both.shape[1] // 2
    row = lax.broadcasted_iota(jnp.int32, (PAIR, size), 0)
    return jnp.where(row < HD, both[:, :size], both[:, size:])


def unit_of(size):
    r = lax.broadcasted_iota(jnp.int32, (size, size), 0)
    c = lax.broadcasted_iota(jnp.int32, (size, size), 1)
    return (r == c).astype(F32).astype(BF16)


def attend_kernel(plan, len_ref, acts_ref, bias_ref, *refs):
    weights, (qkv_ref, ctx_ref, lse_ref, mask_ref) = refs[:-4], refs[-4:]
    rows, own = ctx_ref.shape
    write_mask(len_ref, mask_ref)
    for at in range(0, 3 * own, own):
        cut = slice(at, at + own)
        qkv_ref[:, cut] = (dot_nn(acts_ref[...], stacked(weights, plan, cut)) + bias_ref[:, cut]).astype(BF16)
    unit = unit_of(PAIR)
    scale = jnp.asarray(HD**-0.5, BF16)
    for pair in range(own // PAIR):
        at = pair * PAIR
        keys = qkv_ref[:, own + at : own + at + PAIR]
        values_t = dot_nt(unit, qkv_ref[:, 2 * own + at : 2 * own + at + PAIR]).astype(BF16)
        for lo, hi in row_blocks(rows):
            size = hi - lo
            both = both_heads(qkv_ref[lo:hi, at : at + PAIR] * scale)
            mask = mask_ref[:hi, lo:hi]
            scores = dot_nt(keys[:hi], both) + jnp.concatenate([mask, mask], axis=1)
            peak = jnp.max(scores, axis=0, keepdims=True)
            expo = jnp.exp(scores - peak)
            total = jnp.sum(expo, axis=0, keepdims=True)
            probs = (expo * (1.0 / total)).astype(BF16)
            lse = peak + jnp.log(total)
            lse_ref[2 * pair : 2 * pair + 1, lo:hi] = lse[:, :size]
            lse_ref[2 * pair + 1 : 2 * pair + 2, lo:hi] = lse[:, size:]
            ctx_ref[lo:hi, at : at + PAIR] = own_rows(dot_nn(values_t[:, :hi], probs)).T.astype(BF16)


def middle_kernel(lo, plan, many, rank_ref, order_ref, row_ref, bup_ref, ctx_ref, ent_ref, gbm_ref, *refs):
    weights, downs, (mid_ref, acts_ref, active_ref, ghid_ref, gn_ref, gbup_ref) = refs[:many], refs[many:-6], refs[-6:]
    plan, plan_dn = plan
    rows = slice(lo, lo + mid_ref.shape[0])
    zero = rank_ref[0, 0] == 0
    own = ctx_ref.shape[1] // 2
    last = last_of(order_ref)

    def ordered(a, b):
        return jnp.where(zero, a, b), jnp.where(zero, b, a)

    w_first, w_second = ordered(stacked(weights, plan, slice(0, own)), stacked(weights, plan, slice(own, 2 * own)))
    branch = dot_nt(ctx_ref[rows, :own], w_first) + dot_nt(ctx_ref[rows, own:], w_second) + row_ref[2:3]
    middle = ent_ref[rows, :].astype(F32) + center(branch) * (1.0 - last)
    mid_ref[...] = middle
    normed, _ = norm_of(expand(middle, last))
    acts = (normed * row_ref[1:2]).astype(BF16)
    acts_ref[...] = acts
    gbm = gbm_ref[rows, :]
    units = active_ref.shape[1]
    piece = units // 2
    total = None
    for at in range(0, units, piece):
        cut, cut_up = slice(at, at + piece), slice(2 * own + at, 2 * own + at + piece)
        up_part = stacked(weights, plan, cut_up)
        hidden = dot_nn(acts, up_part) + bup_ref[:, cut]
        gact = dot_nn(gbm, stacked(downs, plan_dn, cut))
        square = hidden * hidden
        bend = jnp.tanh(hidden * (0.7978845608028654 + 0.7978845608028654 * 0.044715 * square))
        up = 0.5 + 0.5 * bend
        active_ref[:, cut] = (hidden * up).astype(BF16)
        slope = up + (0.5 * hidden) * (1.0 - bend * bend) * (
            0.7978845608028654 + 0.7978845608028654 * 3 * 0.044715 * square
        )
        ghid = (gact * slope).astype(BF16)
        ghid_ref[:, cut] = ghid
        gbup_ref[:, cut] = jnp.sum(ghid.astype(F32), axis=0, keepdims=True)
        part = dot_nt(ghid, up_part)
        total = part if total is None else total + part
    gn_ref[...] = total.astype(BF16)


def mix_kernel(plan, parts, *refs):
    refs[-1][...] = dot_nt(joined(refs[:parts]), stacked(refs[parts:-1], plan, slice(None))).astype(BF16)


def back_kernel(lo, plan, order_ref, row_ref, own_ref, other_ref, mid_ref, top_ref, *refs):
    weights, (gmid_ref, gba_ref, gctx_ref, sum_ref) = refs[:-4], refs[-4:]
    last = last_of(order_ref)
    gain = row_ref[1:2]
    weights = stacked(weights, plan, slice(0, gctx_ref.shape[1]))

    def one(at, carry):
        grad = own_ref[at, :].astype(F32) + other_ref[at, :].astype(F32)
        normed, inverse = norm_of(expand(mid_ref[at, :], last))
        gmid = top_ref[at, :].astype(F32) + norm_backward(grad, normed, inverse, gain, last)
        gmid_ref[at, :] = gmid
        gba = center(gmid)
        low = gba.astype(BF16)
        gba_ref[at, :] = low
        gctx_ref[at, :] = dot_nn(low, weights).astype(BF16)
        gain_sum, ba_sum = carry
        return (
            gain_sum + jnp.sum(grad * normed, axis=0, keepdims=True),
            ba_sum + jnp.sum(gba, axis=0, keepdims=True),
        )

    zero = jnp.zeros((1, sum_ref.shape[1]), F32)
    sum_ref[0:1, :], sum_ref[1:2, :] = by_rows(own_ref.shape[0], one, (zero, zero))
    sum_ref[2:, :] = jnp.zeros((sum_ref.shape[0] - 2, sum_ref.shape[1]), F32)


def attend_back_kernel(
    len_ref, qkv_ref, lse_ref, *refs
):
    gctx_refs, (gq_ref, gkv_ref, mask_ref, gk_ref, gv_ref) = refs[:-5], refs[-5:]
    rows, own = gq_ref.shape
    write_mask(len_ref, mask_ref)
    unit = unit_of(PAIR)
    scale = jnp.asarray(HD**-0.5, BF16)
    for pair in range(own // PAIR):
        at = pair * PAIR
        keys = qkv_ref[:, own + at : own + at + PAIR]
        values = qkv_ref[:, 2 * own + at : 2 * own + at + PAIR]
        keys_t = dot_nt(unit, keys * scale).astype(BF16)
        gctx = joined(gctx_refs, slice(at, at + PAIR))
        for lo, hi in reversed(row_blocks(rows)):
            size = hi - lo
            both_q = both_heads(qkv_ref[lo:hi, at : at + PAIR] * scale)
            both_g = both_heads(gctx[lo:hi])
            lse = jnp.concatenate(
                [lse_ref[2 * pair : 2 * pair + 1, lo:hi], lse_ref[2 * pair + 1 : 2 * pair + 2, lo:hi]], axis=1
            )
            mask = mask_ref[:hi, lo:hi]
            probs = jnp.exp(dot_nt(keys[:hi], both_q) + jnp.concatenate([mask, mask], axis=1) - lse)
            gprobs = dot_nt(values[:hi], both_g)
            delta = jnp.sum(probs * gprobs, axis=0, keepdims=True)
            gscores = (probs * (gprobs - delta)).astype(BF16)
            gq_ref[lo:hi, at : at + PAIR] = own_rows(dot_nn(keys_t[:, :hi], gscores)).T.astype(BF16)
            gk = dot_nn(gscores, both_q)
            gv = dot_nn(probs.astype(BF16), both_g)
            if hi == rows:
                gk_ref[...] = gk
                gv_ref[...] = gv
            else:
                gk_ref[:hi, :] += gk
                gv_ref[:hi, :] += gv
        gkv_ref[:, at : at + PAIR] = gk_ref[...].astype(BF16)
        gkv_ref[:, own + at : own + at + PAIR] = gv_ref[...].astype(BF16)


def part_kernel(plan, gq_ref, gkv_ref, ent_ref, order_ref, *refs):
    weights, (part_ref, sum_ref, bias_ref) = refs[:-3], refs[-3:]
    own = gq_ref.shape[1]
    last = last_of(order_ref)
    w_q, w_kv = stacked(weights, plan, slice(0, own)), stacked(weights, plan, slice(own, 3 * own))

    def one(at, carry):
        gq, gkv = gq_ref[at, :], gkv_ref[at, :]
        part = (dot_nt(gq, w_q) + dot_nt(gkv, w_kv)).astype(BF16)
        part_ref[at, :] = part
        normed, _ = norm_of(expand(ent_ref[at, :].astype(F32), last))
        gain_sum, q_sum, v_sum = carry
        return (
            gain_sum + jnp.sum(part.astype(F32) * normed, axis=0, keepdims=True),
            q_sum + jnp.sum(gq.astype(F32), axis=0, keepdims=True),
            v_sum + jnp.sum(gkv[:, own:].astype(F32), axis=0, keepdims=True),
        )

    zeros = jnp.zeros((1, 2 * own), F32), jnp.zeros((1, own), F32), jnp.zeros((1, own), F32)
    sum_ref[...], bias_ref[:, :own], bias_ref[:, own:] = by_rows(gq_ref.shape[0], one, zeros)


def vector_kernel(parts, order_ref, row_ref, gain_ref, gain_other, bias_ref, *refs):
    sum_refs, gbup_refs, out_ref = refs[:parts], refs[parts:-1], refs[-1]
    width = order_ref.shape[1]
    chooser = chooser_of(order_ref, width)
    sums = sum(ref[0:2] for ref in sum_refs)
    gbup = sum(ref[...] for ref in gbup_refs)
    gain = gain_ref[...] + gain_other[...]
    rows = jnp.concatenate([row_ref[4:5], sums, gain, jnp.zeros((4, width), F32)], axis=0)
    plain = jnp.zeros_like(rows)
    for _ in range(3):
        low = rows.astype(BF16)
        plain = plain + dot_nt(low, chooser)
        rows = rows - low.astype(F32)
    plain = jnp.concatenate([plain[0:4], gbup[:, :width], gbup[:, width:], bias_ref[...], plain[7:8]], axis=0)
    lanes = out_ref.shape[1]
    for r in range(8):
        for j in range(width // lanes):
            at = r * (width // lanes) + j
            out_ref[at : at + 1, :] = plain[r : r + 1, j * lanes : (j + 1) * lanes]


def result_kernel(order_ref, row_ref, mid_ref, own_ref, other_ref, out_ref, chooser_ref):
    last = last_of(order_ref)
    chooser_ref[...] = chooser_of(order_ref, order_ref.shape[1])

    def one(at, carry):
        branch = own_ref[at, :].astype(F32) + other_ref[at, :].astype(F32) + row_ref[3:4]
        result = (mid_ref[at, :] + center(branch) * (1.0 - last)).astype(BF16)
        out_ref[at, :] = dot_nt(result, chooser_ref[...])[:, : out_ref.shape[1]].astype(BF16)
        return carry

    by_rows(mid_ref.shape[0], one)


def final_kernel(order_ref, row_ref, own_ref, other_ref, ent_ref, gmid_ref, out_ref, chooser_ref):
    last = last_of(order_ref)
    chooser_ref[...] = chooser_of(order_ref, order_ref.shape[1])

    def one(at, carry):
        grad = own_ref[at, :].astype(F32) + other_ref[at, :].astype(F32)
        normed, inverse = norm_of(expand(ent_ref[at, :].astype(F32), last))
        grad = (gmid_ref[at, :] + norm_backward(grad, normed, inverse, row_ref[0:1], last)).astype(BF16)
        out_ref[at, :] = dot_nt(grad, chooser_ref[...])[:, : out_ref.shape[1]].astype(BF16)
        return carry

    by_rows(ent_ref.shape[0], one)


def pairs_of(refs, counts):
    found, at = [], 0
    for acts, grads in counts:
        found.append((refs[at : at + acts], refs[at + acts : at + acts + grads]))
        at += acts + grads
    return found


def send_kernel(counts, pieces, *refs):
    outs, at = refs[-pieces:], 0
    rows = outs[0].shape[0]
    for acts, grads in pairs_of(refs, counts):
        half = acts[0].shape[1] // 2
        cut = slice(at, at + grads[0].shape[1])
        made = dot_tn(joined(acts, slice(half, None)), joined(grads)).astype(BF16)
        for i, out_ref in enumerate(outs):
            out_ref[:, cut] = made[i * rows : (i + 1) * rows]
        at += grads[0].shape[1]


def keep_kernel(counts, pieces, radix, each, *refs):
    many = (radix - 1) * each
    keep_ref, send_refs = refs[-many - 1], refs[len(refs) - many :]
    got = joined(refs[-many - 1 - pieces : -many - 1]).astype(F32)
    rows, at = keep_ref.shape[0], 0
    size = rows // each
    for acts, grads in pairs_of(refs, counts):
        cut = slice(at, at + grads[0].shape[1])
        half = dot_tn(joined(acts, slice(0, rows * radix)), joined(grads)) + got[:, cut]
        keep_ref[:, cut] = half[:rows]
        for k, send_ref in enumerate(send_refs):
            send_ref[:, cut] = half[rows + k * size : rows + (k + 1) * size].astype(BF16)
        at += grads[0].shape[1]


def add_kernel(given, each, *refs):
    total = refs[0][...]
    for i in range(1, 1 + given, each):
        total = total + joined(refs[i : i + each]).astype(F32)
    rows = refs[1 + given].shape[0]
    refs[1 + given][...] = total[:rows]
    for k, ref in enumerate(refs[2 + given :]):
        ref[...] = total[(k + 1) * rows : (k + 2) * rows].astype(BF16)


def add_vector_kernel(given, each, *refs):
    vector, refs = refs[0][...].astype(BF16), refs[1:]
    total = refs[0][...]
    for i in range(1, 1 + given, each):
        total = total + joined(refs[i : i + each]).astype(F32)
    rows, columns = refs[1 + given].shape
    refs[1 + given][...] = total[:rows]
    for k, ref in enumerate(refs[2 + given :]):
        ref[:, :columns] = total[(k + 1) * rows : (k + 2) * rows].astype(BF16)
        ref[:, columns:] = vector


def finish_kernel(given, vectors, vector_ref, keep_ref, *refs):
    got, cuts, vec_refs = refs[:given], refs[given:-vectors], refs[-vectors:]
    columns = keep_ref.shape[1]
    total = keep_ref[...]
    parts = [vector_ref[...].astype(BF16).astype(F32)]
    for ref in got:
        total = total + ref[:, :columns].astype(F32)
        parts.append(ref[:, columns:].astype(F32))
    at = 0
    for ref in cuts:
        ref[...] = total[:, at : at + ref.shape[1]]
        at += ref.shape[1]
    while len(parts) > 1:
        parts = [parts[i] + parts[i + 1] for i in range(0, len(parts), 2)]
    at, lanes = 0, parts[0].shape[1]
    for ref in vec_refs:
        for j in range(ref.shape[0] // lanes):
            ref[j * lanes : (j + 1) * lanes] = parts[0][at]
            at += 1


def gather_far(shard, count):
    return jnp.concatenate(gather_far_pieces(shard, count), axis=0)


def gather_far_pieces(shard, count):
    pieces = [shard]
    for stride, radix in reversed(phases_of(count)[2:]):
        held = pieces[0] if len(pieces) == 1 else jnp.concatenate(pieces, axis=0)
        pieces = [held] + [swap(held, k * stride) for k in range(1, radix)]
    return pieces


def gather_near(held, count):
    pieces = [held]
    for stride, radix in phases_of(count)[1:2]:
        pieces += [swap(held, k * stride) for k in range(1, radix)]
    return pieces


def plan_of(pieces):
    return tuple((i, 0, piece.shape[0]) for i, piece in enumerate(pieces))


def near_first(shard, count):
    middle = shard.shape[1] // 2
    halves = [shard[:, :middle], shard[:, middle:]]
    if len(phases_of(count)) != 3:
        return halves
    return [piece for pair in zip(*(gather_near(half, count) for half in halves)) for piece in pair]


def then_far(held, count):
    phases = phases_of(count)
    if len(phases) != 3:
        pieces = gather_near(gather_far(held, count), count)
        return pieces, plan_of(pieces + pieces)
    (_, near), (stride, far) = phases[1:]
    rows = held.shape[0] // near
    pieces = [held] + [swap(held, k * stride) for k in range(1, far)]
    plan = [(core * far + z, x * rows, rows) for core in range(2) for x in range(near) for z in range(far)]
    return pieces, tuple(plan)


class Sum:
    def __init__(self, pairs, count, first=4, second=1):
        self.flat = [a for pair in pairs for parts in pair for a in parts]
        self.counts = tuple((len(acts), len(grads)) for acts, grads in pairs)
        self.phases = phases_of(count)
        self.columns = sum(grads[0].shape[1] for _, grads in pairs)
        self.rows = pairs[0][0][0].shape[1] // 2
        self.each, self.second = first, second
        self.sent = call(
            functools.partial(send_kernel, self.counts, first),
            [shape(self.rows // first, self.columns, BF16)] * first,
            self.flat,
        )
        self.keep = None
        self.got = []

    def go(self):
        (stride, _), self.phases = self.phases[0], self.phases[1:]
        self.got = [swap(piece, (k // self.each + 1) * stride) for k, piece in enumerate(self.sent)]
        return self

    def work(self):
        got = self.got
        if not self.phases:
            total = self.keep
            for piece in got:
                total = total + piece.astype(F32)
            self.keep = total
            return self
        radix = self.phases[0][1]
        self.rows //= radix
        outs = [shape(self.rows, self.columns, F32)]
        if self.keep is None:
            each = self.second if self.rows % (16 * self.second) == 0 else 1
            outs += [shape(self.rows // each, self.columns, BF16)] * ((radix - 1) * each)
            kernel = functools.partial(keep_kernel, self.counts, len(got), radix, each)
            outs = call(kernel, outs, self.flat + got)
        elif self.rows % 16 == 0:
            outs += [shape(self.rows, self.columns, BF16)] * (radix - 1)
            outs = call(functools.partial(add_kernel, len(got), self.each), outs, [self.keep] + got)
            each = 1
        else:
            total = self.keep
            for i in range(0, len(got), self.each):
                total = total + jnp.concatenate(got[i : i + self.each], axis=0).astype(F32)
            parts = [total[k * self.rows : (k + 1) * self.rows] for k in range(radix)]
            outs = [parts[0]] + [part.astype(BF16) for part in parts[1:]]
            each = 1
        self.each = each
        self.keep, *self.sent = outs
        return self

    def end(self):
        while self.phases:
            self.go().work()
        return self.keep


def tie(sums, *arrays):
    flat = list(arrays) + [piece for one in sums for piece in one.got]
    flat = lax.optimization_barrier(tuple(flat))
    at = len(arrays)
    for one in sums:
        one.got = list(flat[at : at + len(one.got)])
        at += len(one.got)
    return flat[: len(arrays)]


def flips_of(phases):
    found = [0]
    for stride, radix in phases:
        found = [k * stride + f for k in range(radix) for f in found]
    return found[1:]


def reduce_all(vector, flips):
    return total_of([vector] + [swap(vector, flip) for flip in flips])


def total_of(parts):
    while len(parts) > 1:
        parts = [parts[i] + parts[i + 1] for i in range(0, len(parts), 2)]
    return parts[0]


def body(
    stream,
    w_query,
    w_key,
    w_value,
    b_query,
    b_value,
    w_out,
    b_out,
    gain_attn,
    w_up,
    b_up,
    w_down,
    b_down,
    gain_mlp,
    cotangent,
    lengths,
):
    rows, inner_width = stream.shape
    count = lax.axis_size("dp")
    me = lax.axis_index("dp")
    rank = lax.axis_index("tensor").astype(jnp.int32).reshape(1, 1)
    shard_rows, own = w_query.shape
    width = shard_rows * count
    units = w_up.shape[1]
    blocks = jnp.array(relative_order(count), jnp.int32)
    order = ((me ^ blocks)[:, None] * shard_rows + jnp.arange(shard_rows, dtype=jnp.int32)).reshape(1, -1)

    shard_qkv = pack([w_query, w_key, w_value], 56 * 1024 * 1024)
    qkv_far = gather_far_pieces(shard_qkv, count)
    w_out_t, w_up, shard_dn, order, rank = lax.optimization_barrier((w_out.T, w_up, w_down.T, order, rank, shard_qkv))[:5]
    shard_ou = pack([w_out_t, swap_tensor(w_out_t), w_up])
    ent, acts_a = call(
        first_kernel,
        [shape(rows, width, BF16)] * 2,
        [order, stream, gain_attn],
        scratch=[pltpu.VMEM((width, width), BF16)],
    )
    dn_near = near_first(shard_dn, count)
    flat = lax.optimization_barrier((shard_ou, acts_a, *qkv_far, *dn_near))
    shard_ou, acts_a, qkv_far, dn_near = flat[0], flat[1], flat[2 : 2 + len(qkv_far)], flat[2 + len(qkv_far) :]
    middle_at = (len(qkv_far) + 1) // 2
    halves = [jnp.concatenate(part, axis=0) for part in (qkv_far[:middle_at], qkv_far[middle_at:]) if part]
    qkv_w = [piece for group in zip(*(gather_near(half, count) for half in halves)) for piece in group]
    ou_far = gather_far_pieces(shard_ou, count)

    qkv_w = qkv_w + [swap(piece, 1) for piece in qkv_w]
    plan = plan_of(qkv_w)
    bias_qkv = jnp.concatenate([b_query, jnp.zeros_like(b_query), b_value]).astype(F32)[None]
    qkv, context, lse = call(
        functools.partial(attend_kernel, plan),
        [shape(rows, 3 * own, BF16), shape(rows, own, BF16), shape(8, rows, F32)],
        [lengths, acts_a, bias_qkv] + qkv_w,
        scalars=1,
        scratch=[pltpu.VMEM((rows, rows), F32)],
    )
    context, *ou_far = lax.optimization_barrier((context, *ou_far))
    dn_near = jnp.concatenate([jnp.concatenate(dn_near[i::2], axis=0) for i in range(2)], axis=1)
    ou_far = jnp.concatenate(ou_far, axis=0)
    other_context = [swap_tensor(context)]
    ou_w = gather_near(ou_far, count)
    dn_w, plan_dn = then_far(dn_near, count)
    made = call(
        prepare_kernel,
        [shape(rows, width, BF16)] * 4 + [shape(8, width, F32)],
        [rank, order, cotangent, context, *other_context, ent, gain_attn, gain_mlp, b_out, b_down],
        scalars=1,
    )
    flat = lax.optimization_barrier((*made, *ou_w, *dn_w))
    (context_all, ent_mid, top, gbm, row), flat = flat[:5], flat[5:]
    ou_w, dn_w = list(flat[: len(ou_w)]), list(flat[len(ou_w) :])
    ou_w = ou_w + [swap(piece, 1) for piece in ou_w]
    plan_ou = plan_of(ou_w)
    dn_w = dn_w + [swap(piece, 1) for piece in dn_w]

    cuts = [(0, rows)]
    bias_up = b_up.astype(F32)[None]
    middle, acts_m, active, ghid, gn, gn_other, gbup = [], [], [], [], [], [], []
    for lo, size in cuts:
        made = call(
            functools.partial(middle_kernel, lo, (plan_ou, plan_dn), len(ou_w)),
            [
                shape(size, width, F32),
                shape(size, width, BF16),
                shape(size, units, BF16),
                shape(size, units, BF16),
                shape(size, width, BF16),
                shape(1, units, F32),
            ],
            [rank, order, row, bias_up, context_all, ent_mid, gbm] + ou_w + dn_w,
            scalars=1,
        )
        for held, new in zip((middle, acts_m, active, ghid, gn, gbup), made):
            held.append(new)
        gn_other.append(swap_tensor(gn[-1]))

    sum_dn = Sum([((gbm,), active)], count, first=2).go()
    sum_up = Sum([(acts_m, ghid)], count, first=2).go()
    sum_dn.work().go()
    sum_up.work().go()
    (mlp,) = call(
        functools.partial(mix_kernel, plan_dn, len(active)),
        [shape(rows, width, BF16)],
        [after(active[0], sum_up.sent)] + active[1:] + dn_w,
    )
    mlp_other = swap_tensor(mlp)
    sum_dn.work().go()

    gmid, gba, gctx, sums = [], [], [], []
    gn_other[0] = after(gn_other[0], sum_dn.sent, sum_up.sent, mlp)
    for i, (lo, size) in enumerate(cuts):
        made = call(
            functools.partial(back_kernel, lo, plan_ou),
            [shape(size, width, F32), shape(size, width, BF16), shape(size, own, BF16), shape(8, width, F32)],
            [order, row, gn[i], gn_other[i], middle[i], top] + ou_w,
        )
        for held, new in zip((gmid, gba, gctx, sums), made):
            held.append(new)
    gq, gkv = call(
        attend_back_kernel,
        [shape(rows, own, BF16), shape(rows, 2 * own, BF16)],
        [lengths, qkv, lse] + gctx,
        scalars=1,
        scratch=[pltpu.VMEM((rows, rows), F32), pltpu.VMEM((rows, PAIR), F32), pltpu.VMEM((rows, PAIR), F32)],
        cost=LONG,
    )
    gq, gkv = tie([sum_dn, sum_up], gq, gkv)
    sum_last = Sum([(gba, (context,)), ((acts_a,), (gq,)), ((acts_a,), (gkv,))], count, first=2).go()
    sum_last.work().go()
    sum_up.work().go()
    gq, gkv, mlp_other = lax.optimization_barrier((gq, gkv, mlp_other, *sum_last.sent, *sum_up.sent))[:3]
    part, gain, gbias = call(
        functools.partial(part_kernel, plan),
        [shape(rows, width, BF16), shape(1, width, F32), shape(1, 2 * own, F32)],
        [gq, gkv, ent, order] + qkv_w,
        cost=LONG,
    )
    gain_other = swap_tensor(gain)
    part_other = swap_tensor(part)
    (plain,) = call(
        functools.partial(vector_kernel, len(cuts)),
        [shape(8 * width // 128, 128, F32)],
        [order, row, gain, gain_other, gbias] + sums + gbup,
    )
    phases = phases_of(count)
    parts = [plain] + [swap(plain, flip) for flip in flips_of(phases[:2])]
    plain = total_of(list(tie([sum_last, sum_up], *parts)))
    short = len(phases) == 3
    if short:
        block = plain
        given, radix, size = len(sum_last.got), phases[2][1], sum_last.rows // phases[2][1]
        columns = sum_last.columns
        keep, *sent = call(
            functools.partial(add_vector_kernel, given, sum_last.each),
            [shape(size, columns, F32)] + [shape(size, columns + block.shape[1], BF16)] * (radix - 1),
            [block, sum_last.keep] + sum_last.got,
        )
        last_got = [swap(piece, (k + 1) * phases[2][0]) for k, piece in enumerate(sent)]
    else:
        sum_last.work()
        sent = sum_last.sent
        sum_last.go()
        for phase in phases[2:]:
            plain = reduce_all(plain, flips_of([phase]))
    mlp_other = after(mlp_other, sent)
    (out_rows,) = call(
        result_kernel,
        [shape(rows, inner_width, BF16)],
        [order, row, *middle, mlp, mlp_other],
        scratch=[pltpu.VMEM((width, width), BF16)],
    )
    part_other, out_rows = lax.optimization_barrier((part_other, out_rows))
    (grad_stream,) = call(
        final_kernel,
        [shape(rows, inner_width, BF16)],
        [order, row, part, part_other, ent, *gmid],
        scratch=[pltpu.VMEM((width, width), BF16)],
    )
    shard_dn_t, shard_up = (one.work().end() for one in (sum_dn, sum_up))
    if short:
        keep, grad_stream = lax.optimization_barrier((keep, grad_stream))
        sizes = [width] * 4 + [2 * width, own, own]
        out_t, grad_q, grad_k, grad_v, *vectors = call(
            functools.partial(finish_kernel, len(last_got), len(sizes)),
            [shape(shard_rows, own, F32)] * 4 + [jax.ShapeDtypeStruct((size,), F32) for size in sizes],
            [block, keep] + last_got,
        )
    else:
        last = sum_last.work().end()
        out_t, grad_q, grad_k, grad_v = (last[:, i * own : (i + 1) * own] for i in range(4))
        plain = plain.reshape(8, width)
        vectors = [plain[0], plain[1], plain[2], plain[3], plain[4:6].reshape(-1), plain[6, :own], plain[6, own:]]
    grad_b_down, grad_gain_mlp, grad_b_out, grad_gain_attn, grad_b_up, grad_b_query, grad_b_value = vectors
    return (
        out_rows,
        grad_stream,
        grad_q,
        grad_k,
        grad_v,
        grad_b_query,
        grad_b_value,
        out_t.T,
        grad_b_out,
        grad_gain_attn,
        shard_up,
        grad_b_up,
        shard_dn_t.T,
        grad_b_down,
        grad_gain_mlp,
    )


def solution(mesh):
    return jax.shard_map(
        body,
        mesh=mesh,
        in_specs=(
            P("dp", None),
            P("dp", "tensor"),
            P("dp", "tensor"),
            P("dp", "tensor"),
            P("tensor"),
            P("tensor"),
            P("tensor", "dp"),
            P(),
            P(),
            P("dp", "tensor"),
            P("tensor"),
            P("tensor", "dp"),
            P(),
            P(),
            P("dp", None),
            P("dp", None),
        ),
        out_specs=(
            P("dp", None),
            P("dp", None),
            P("dp", "tensor"),
            P("dp", "tensor"),
            P("dp", "tensor"),
            P("tensor"),
            P("tensor"),
            P("tensor", "dp"),
            P(),
            P(),
            P("dp", "tensor"),
            P("tensor"),
            P("tensor", "dp"),
            P(),
            P(),
        ),
        check_vma=False,
    )
```

profile of v0, /device:TPU:8, one launch (start us, length us, event | category | flops | bytes accessed | tf_op | source)
XLA Modules:
  0.0 162.9 jit_solution(15699775950174883005)
XLA Ops:
  2.3 3.0 %collective-permute-start.2 = (bf16[48,1152]{1,0:T(8,128)(2,1)}, bf16[48,1152]{1,0:T(8,128)(2,1)S(1)}, u32[]{:S(2)}, u32[]{:S(2)}) collective-permute-start(bf16[48,1152]{1,0:T(8,128)(2,1)} %shard_map.280), channel_id=1, source_target_pairs={{0,16},{2,18},{4,20},{6,22},{8,24},{10,26},{12,28},{14,30},{16,0},... | collective-permute-start | bytes 331784 | tf_op jit(solution)/shard_map/ppermute | solution.py:42
  14.1 2.3 %shard_map.282 = (bf16[576,768]{1,0:T(8,128)(2,1)S(1)}, bf16[576,768]{1,0:T(8,128)(2,1)S(1)}) custom-call(s32[1,768]{1,0:T(1,128)S(1)} %add.53.order_ref, bf16[576,767]{1,0:T(8,128)(2,1)S(1)} %copy-done.1, bf16[768]{0:T(1024)(128)(2,1)S(1)} %copy-done.6), custom_call_target="tpu_custom_call" | custom-call | bytes 1024 | tf_op jit(solution)/shard_map/pallas_call | solution.py:71
  22.5 3.2 %collective-permute-done.7.refs_3_ = bf16[96,1152]{1,0:T(8,128)(2,1)S(1)} collective-permute-done((bf16[96,1152]{1,0:T(8,128)(2,1)S(1)}, bf16[96,1152]{1,0:T(8,128)(2,1)S(1)}, u32[]{:S(2)}, u32[]{:S(2)}) %collective-permute-start.7) | collective-permute-done | bytes 221216 | tf_op jit(solution)/shard_map/ppermute | solution.py:42
  25.6 3.5 %collective-permute-start.13 = (bf16[48,2304]{1,0:T(8,128)(2,1)S(1)}, bf16[48,2304]{1,0:T(8,128)(2,1)S(1)}, u32[]{:S(2)}, u32[]{:S(2)}) collective-permute-start(bf16[48,2304]{1,0:T(8,128)(2,1)S(1)} %shard_map.281), channel_id=1, source_target_pairs={{0,16},{2,18},{4,20},{6,22},{8,24},{10,26},{12,28},{14,30},{16,0},... | collective-permute-start | bytes 663560 | tf_op jit(solution)/shard_map/ppermute | solution.py:42
  31.7 5.9 %shard_map.283 = (bf16[576,1152]{1,0:T(8,128)(2,1)S(1)}, bf16[576,384]{1,0:T(8,128)(2,1)S(1)}, f32[8,576]{1,0:T(8,128)S(1)}) custom-call(s32[1,4]{1,0:T(1,128)S(1)} %copy-done.11, bf16[576,768]{1,0:T(8,128)(2,1)S(1)} %get-tuple-element.135.acts_ref.refs_2_.refs_4_, f32[1,1152]{1,0:T(1,128)S(1)} %fusion.1.bias_ref, ...), custom_call_target="tpu_custom_call" | custom-call | bytes 1024 | tf_op jit(solution)/shard_map/pallas_call | solution.py:71
  37.7 3.8 %collective-permute-done.13 = bf16[48,2304]{1,0:T(8,128)(2,1)S(1)} collective-permute-done((bf16[48,2304]{1,0:T(8,128)(2,1)S(1)}, bf16[48,2304]{1,0:T(8,128)(2,1)S(1)}, u32[]{:S(2)}, u32[]{:S(2)}) %collective-permute-start.13) | collective-permute-done | bytes 221216 | tf_op jit(solution)/shard_map/ppermute | solution.py:42
  41.4 3.3 %collective-permute-done.14 = bf16[48,2304]{1,0:T(8,128)(2,1)S(1)} collective-permute-done((bf16[48,2304]{1,0:T(8,128)(2,1)S(1)}, bf16[48,2304]{1,0:T(8,128)(2,1)S(1)}, u32[]{:S(2)}, u32[]{:S(2)}) %collective-permute-start.14) | collective-permute-done | bytes 221216 | tf_op jit(solution)/shard_map/ppermute | solution.py:42
  47.1 3.0 %collective-permute-start.18 = (bf16[96,1536]{1,0:T(8,128)(2,1)S(1)}, bf16[96,1536]{1,0:T(8,128)(2,1)S(1)}, u32[]{:S(2)}, u32[]{:S(2)}) collective-permute-start(bf16[96,1536]{1,0:T(8,128)(2,1)S(1)} %maximum_maximum_fusion.refs_4_.refs_1_), channel_id=1, source_target_pairs={{0,16},{2,18},{4,20},{6,22},{8,24},{10,26},{12,28},{14,30},{16,0},... | collective-permute-start | bytes 884744 | tf_op jit(solution)/shard_map/ppermute | solution.py:42
  50.6 3.2 %collective-permute-done.15.other_ref = bf16[576,384]{1,0:T(8,128)(2,1)S(1)} collective-permute-done((bf16[576,384]{1,0:T(8,128)(2,1)S(1)}, bf16[576,384]{1,0:T(8,128)(2,1)S(1)}, u32[]{:S(2)}, u32[]{:S(2)}) %collective-permute-start.15) | collective-permute-done | bytes 442400 | tf_op jit(solution)/shard_map/ppermute | solution.py:47
  57.0 10.5 %collective-permute-done.18.refs_6_.refs_3_ = bf16[96,1536]{1,0:T(8,128)(2,1)S(1)} collective-permute-done((bf16[96,1536]{1,0:T(8,128)(2,1)S(1)}, bf16[96,1536]{1,0:T(8,128)(2,1)S(1)}, u32[]{:S(2)}, u32[]{:S(2)}) %collective-permute-start.18) | collective-permute-done | bytes 294944 | tf_op jit(solution)/shard_map/ppermute | solution.py:42
  67.5 4.5 %collective-permute-done.19.refs_7_.refs_4_ = bf16[96,1536]{1,0:T(8,128)(2,1)S(1)} collective-permute-done((bf16[96,1536]{1,0:T(8,128)(2,1)S(1)}, bf16[96,1536]{1,0:T(8,128)(2,1)S(1)}, u32[]{:S(2)}, u32[]{:S(2)}) %collective-permute-start.19) | collective-permute-done | bytes 294944 | tf_op jit(solution)/shard_map/ppermute | solution.py:42
  73.1 3.1 %collective-permute-done.22.refs_8_.refs_5_ = bf16[96,1536]{1,0:T(8,128)(2,1)S(1)} collective-permute-done((bf16[96,1536]{1,0:T(8,128)(2,1)S(1)}, bf16[96,1536]{1,0:T(8,128)(2,1)S(1)}, u32[]{:S(2)}, u32[]{:S(2)}) %collective-permute-start.22) | collective-permute-done | bytes 294944 | tf_op jit(solution)/shard_map/ppermute | solution.py:42
  77.7 7.2 %shard_map.285 = (f32[576,768]{1,0:T(8,128)S(1)}, bf16[576,768]{1,0:T(8,128)(2,1)S(1)}, bf16[576,1536]{1,0:T(8,128)(2,1)S(1)}, bf16[576,1536]{1,0:T(8,128)(2,1)S...) custom-call(s32[1,1]{1,0:T(1,128)} %bitcast.2.rank_ref, s32[1,768]{1,0:T(1,128)S(1)} %add.53.order_ref, ...), custom_call_target="tpu_custom_call" | custom-call | bytes 1024 | tf_op jit(solution)/shard_map/pallas_call | solution.py:71
  97.1 9.3 %collective-permute-done.29.refs_1_ = bf16[192,1536]{1,0:T(8,128)(2,1)S(1)} collective-permute-done((bf16[192,1536]{1,0:T(8,128)(2,1)S(1)}, bf16[192,1536]{1,0:T(8,128)(2,1)S(1)}, u32[]{:S(2)}, u32[]{:S(2)}) %collective-permute-start.29) | collective-permute-done | bytes 589856 | tf_op jit(solution)/shard_map/ppermute | solution.py:42
  106.6 3.7 %collective-permute-start.33 = (bf16[48,1536]{1,0:T(8,128)(2,1)S(1)}, bf16[48,1536]{1,0:T(8,128)(2,1)S(1)}, u32[]{:S(2)}, u32[]{:S(2)}) collective-permute-start(bf16[48,1536]{1,0:T(8,128)(2,1)S(1)} %get-tuple-element.177), channel_id=1, source_target_pairs={{0,16},{2,18},{4,20},{6,22},{8,24},{10,26},{12,28},{14,30},{16,0},... | collective-permute-start | bytes 442376 | tf_op jit(solution)/shard_map/ppermute | solution.py:42
  111.4 3.0 %shard_map.292 = (f32[576,768]{1,0:T(8,128)S(1)}, bf16[576,768]{1,0:T(8,128)(2,1)S(1)}, bf16[576,384]{1,0:T(8,128)(2,1)S(1)}, f32[8,768]{1,0:T(8,128)S(1)}) custom-call(s32[1,768]{1,0:T(1,128)S(1)} %add.53.order_ref, f32[8,768]{1,0:T(8,128)S(1)} %get-tuple-element.160.row_ref, bf16[576,768]{1,0:T(8,128)(2,1)S(1)} %get-tuple-element.170.own_ref, ...), custom_call_target="tpu_custom_call" | custom-call | bytes 1024 | tf_op jit(solution)/shard_map/pallas_call | solution.py:71
  114.4 6.2 %shard_map.293 = (bf16[576,384]{1,0:T(8,128)(2,1)S(1)}, bf16[576,768]{1,0:T(8,128)(2,1)S(1)}) custom-call(s32[1,4]{1,0:T(1,128)S(1)} %copy-done.11, bf16[576,1152]{1,0:T(8,128)(2,1)S(1)} %get-tuple-element.140.qkv_ref, f32[8,576]{1,0:T(8,128)S(1)} %get-tuple-element.141.lse_ref, bf16[576,384]{1,0:T(8,128)(2,1)S(1)} %get-tuple-element.188.refs_0_), custom_call_target="tpu_custom_call" | custom-call | flops 99999997952 | bytes 1024 | tf_op jit(solution)/shard_map/pallas_call | solution.py:71
  123.9 3.1 %collective-permute-start.46 = (bf16[48,1536]{1,0:T(8,128)(2,1)S(1)}, bf16[48,1536]{1,0:T(8,128)(2,1)S(1)}, u32[]{:S(2)}, u32[]{:S(2)}) collective-permute-start(bf16[48,1536]{1,0:T(8,128)(2,1)S(1)} %get-tuple-element.200), channel_id=1, source_target_pairs={{0,16},{2,18},{4,20},{6,22},{8,24},{10,26},{12,28},{14,30},{16,0},... | collective-permute-start | bytes 442376 | tf_op jit(solution)/shard_map/ppermute | solution.py:42
  130.3 2.5 %shard_map.297 = (bf16[576,768]{1,0:T(8,128)(2,1)S(1)}, f32[1,768]{1,0:T(1,128)S(1)}, f32[1,768]{1,0:T(1,128)S(1)}) custom-call(bf16[576,384]{1,0:T(8,128)(2,1)S(1)} %get-tuple-element.202.refs_3_.gq_ref, bf16[576,768]{1,0:T(8,128)(2,1)S(1)} %get-tuple-element.203.refs_5_.gkv_ref, bf16[576,768]{1,0:T(8,128)(2,1)S(1)} %get-tuple-element.146.ent_in.ent_ref, ...), custom_call_target="tpu_custom_call" | custom-call | flops 99999997952 | bytes 1024 | tf_op jit(solution)/shard_map/pallas_call | solution.py:71
  134.1 2.3 %collective-permute-done.40.gain_other = f32[1,768]{1,0:T(1,128)S(1)} collective-permute-done((f32[1,768]{1,0:T(1,128)S(1)}, f32[1,768]{1,0:T(1,128)S(1)}, u32[]{:S(2)}, u32[]{:S(2)}) %collective-permute-start.40) | collective-permute-done | bytes 3104 | tf_op jit(solution)/shard_map/ppermute | solution.py:47
  141.4 2.6 %collective-permute-done.42 = f32[48,128]{1,0:T(8,128)S(1)} collective-permute-done((f32[48,128]{1,0:T(8,128)S(1)}, f32[48,128]{1,0:T(8,128)S(1)}, u32[]{:S(2)}, u32[]{:S(2)}) %collective-permute-start.42) | collective-permute-done | bytes 24608 | tf_op jit(solution)/shard_map/ppermute | solution.py:42
  148.6 2.9 %shard_map.300 = bf16[576,767]{1,0:T(8,128)(2,1)} custom-call(s32[1,768]{1,0:T(1,128)S(1)} %add.53.order_ref, f32[8,768]{1,0:T(8,128)S(1)} %copy-done.3, f32[576,768]{1,0:T(8,128)S(1)} %get-tuple-element.186.mid_ref, bf16[576,768]{1,0:T(8,128)(2,1)S(1)} %shard_map.291.own_ref, bf16[576,768]{1,0:T(8,128)(2,1)S(1)} %collective-permute-done.36.other_ref), custom_call_target="tpu_custom_call" | custom-call | bytes 1024 | tf_op jit(solution)/shard_map/pallas_call | solution.py:71
  151.5 4.6 %collective-permute-done.39.other_ref = bf16[576,768]{1,0:T(8,128)(2,1)S(1)} collective-permute-done((bf16[576,768]{1,0:T(8,128)(2,1)S(1)}, bf16[576,768]{1,0:T(8,128)(2,1)S(1)}, u32[]{:S(2)}, u32[]{:S(2)}) %collective-permute-start.39) | collective-permute-done | bytes 884768 | tf_op jit(solution)/shard_map/ppermute | solution.py:47
  156.1 3.9 %shard_map.301 = bf16[576,767]{1,0:T(8,128)(2,1)} custom-call(s32[1,768]{1,0:T(1,128)S(1)} %add.53.order_ref, f32[8,768]{1,0:T(8,128)S(1)} %copy-done.3, bf16[576,768]{1,0:T(8,128)(2,1)S(1)} %get-tuple-element.204.own_ref, bf16[576,768]{1,0:T(8,128)(2,1)S(1)} %collective-permute-done.39.other_ref, bf16[576,768]{1,0:T(8,128)(2,1)S(1)} %get-tuple-element.146.ent_in.ent_ref, ...), custom_call_target="tpu_custom_call" | custom-call | bytes 1024 | tf_op jit(solution)/shard_map/pallas_call | solution.py:71
  (155 shorter events, 61.0 us)
Async XLA Ops:
  2.2 16.0 %collective-permute-start.1 = (bf16[48,1152]{1,0:T(8,128)(2,1)}, bf16[48,1152]{1,0:T(8,128)(2,1)S(1)}, u32[]{:S(2)}, u32[]{:S(2)}) collective-permute-start(bf16[48,1152]{1,0:T(8,128)(2,1)} %shard_map.280), channel_id=1, source_target_pairs={{0,8},{2,10},{4,12},{6,14},{8,0},{10,2},{12,4},{14,6},{16,24},{18,... | collective-permute-start | bytes 331784 | tf_op jit(solution)/shard_map/ppermute | solution.py:42
  2.3 16.0 %collective-permute-start.2 = (bf16[48,1152]{1,0:T(8,128)(2,1)}, bf16[48,1152]{1,0:T(8,128)(2,1)S(1)}, u32[]{:S(2)}, u32[]{:S(2)}) collective-permute-start(bf16[48,1152]{1,0:T(8,128)(2,1)} %shard_map.280), channel_id=1, source_target_pairs={{0,16},{2,18},{4,20},{6,22},{8,24},{10,26},{12,28},{14,30},{16,0},... | collective-permute-start | bytes 331784 | tf_op jit(solution)/shard_map/ppermute | solution.py:42
  5.3 13.0 %collective-permute-start.3 = (bf16[48,1152]{1,0:T(8,128)(2,1)}, bf16[48,1152]{1,0:T(8,128)(2,1)S(1)}, u32[]{:S(2)}, u32[]{:S(2)}) collective-permute-start(bf16[48,1152]{1,0:T(8,128)(2,1)} %shard_map.280), channel_id=1, source_target_pairs={{0,24},{2,26},{4,28},{6,30},{8,16},{10,18},{12,20},{14,22},{16,8},... | collective-permute-start | bytes 331784 | tf_op jit(solution)/shard_map/ppermute | solution.py:42
  21.0 16.6 %collective-permute-start.12 = (bf16[48,2304]{1,0:T(8,128)(2,1)S(1)}, bf16[48,2304]{1,0:T(8,128)(2,1)S(1)}, u32[]{:S(2)}, u32[]{:S(2)}) collective-permute-start(bf16[48,2304]{1,0:T(8,128)(2,1)S(1)} %shard_map.281), channel_id=1, source_target_pairs={{0,8},{2,10},{4,12},{6,14},{8,0},{10,2},{12,4},{14,6},{16,24},{18,... | collective-permute-start | bytes 663560 | tf_op jit(solution)/shard_map/ppermute | solution.py:42
  25.6 15.8 %collective-permute-start.13 = (bf16[48,2304]{1,0:T(8,128)(2,1)S(1)}, bf16[48,2304]{1,0:T(8,128)(2,1)S(1)}, u32[]{:S(2)}, u32[]{:S(2)}) collective-permute-start(bf16[48,2304]{1,0:T(8,128)(2,1)S(1)} %shard_map.281), channel_id=1, source_target_pairs={{0,16},{2,18},{4,20},{6,22},{8,24},{10,26},{12,28},{14,30},{16,0},... | collective-permute-start | bytes 663560 | tf_op jit(solution)/shard_map/ppermute | solution.py:42
  29.1 15.6 %collective-permute-start.14 = (bf16[48,2304]{1,0:T(8,128)(2,1)S(1)}, bf16[48,2304]{1,0:T(8,128)(2,1)S(1)}, u32[]{:S(2)}, u32[]{:S(2)}) collective-permute-start(bf16[48,2304]{1,0:T(8,128)(2,1)S(1)} %shard_map.281), channel_id=1, source_target_pairs={{0,24},{2,26},{4,28},{6,30},{8,16},{10,18},{12,20},{14,22},{16,8},... | collective-permute-start | bytes 663560 | tf_op jit(solution)/shard_map/ppermute | solution.py:42
  44.9 27.2 %collective-permute-start.16 = (bf16[192,2304]{1,0:T(8,128)(2,1)S(1)}, bf16[192,2304]{1,0:T(8,128)(2,1)S(1)}, u32[]{:S(2)}, u32[]{:S(2)}) collective-permute-start(bf16[192,2304]{1,0:T(8,128)(2,1)S(1)} %constant_dynamic-update-slice_fusion.4.refs_0_), channel_id=1, source_target_pairs={{0,4},{2,6},{4,0},{6,2},{8,12},{10,14},{12,8},{14,10},{16,20},{18,... | collective-permute-start | bytes 2654216 | tf_op jit(solution)/shard_map/ppermute | solution.py:42
  47.1 20.4 %collective-permute-start.18 = (bf16[96,1536]{1,0:T(8,128)(2,1)S(1)}, bf16[96,1536]{1,0:T(8,128)(2,1)S(1)}, u32[]{:S(2)}, u32[]{:S(2)}) collective-permute-start(bf16[96,1536]{1,0:T(8,128)(2,1)S(1)} %maximum_maximum_fusion.refs_4_.refs_1_), channel_id=1, source_target_pairs={{0,16},{2,18},{4,20},{6,22},{8,24},{10,26},{12,28},{14,30},{16,0},... | collective-permute-start | bytes 884744 | tf_op jit(solution)/shard_map/ppermute | solution.py:42
  50.1 22.0 %collective-permute-start.19 = (bf16[96,1536]{1,0:T(8,128)(2,1)S(1)}, bf16[96,1536]{1,0:T(8,128)(2,1)S(1)}, u32[]{:S(2)}, u32[]{:S(2)}) collective-permute-start(bf16[96,1536]{1,0:T(8,128)(2,1)S(1)} %maximum_maximum_fusion.refs_4_.refs_1_), channel_id=1, source_target_pairs={{0,24},{2,26},{4,28},{6,30},{8,16},{10,18},{12,20},{14,22},{16,8},... | collective-permute-start | bytes 884744 | tf_op jit(solution)/shard_map/ppermute | solution.py:42
  86.7 23.6 %collective-permute-start.26 = (bf16[576,768]{1,0:T(8,128)(2,1)S(1)}, bf16[576,768]{1,0:T(8,128)(2,1)S(1)}, u32[]{:S(2)}, u32[]{:S(2)}) collective-permute-start(bf16[576,768]{1,0:T(8,128)(2,1)S(1)} %get-tuple-element.170.own_ref), channel_id=1, source_target_pairs={{0,1},{1,0},{2,3},{3,2},{4,5},{5,4},{6,7},{7,6},{8,9},{9,8},{10,11... | collective-permute-start | bytes 2654216 | tf_op jit(solution)/shard_map/ppermute | solution.py:47
  90.1 16.2 %collective-permute-start.29 = (bf16[192,1536]{1,0:T(8,128)(2,1)S(1)}, bf16[192,1536]{1,0:T(8,128)(2,1)S(1)}, u32[]{:S(2)}, u32[]{:S(2)}) collective-permute-start(bf16[192,1536]{1,0:T(8,128)(2,1)S(1)} %get-tuple-element.175), channel_id=1, source_target_pairs={{0,4},{2,6},{4,0},{6,2},{8,12},{10,14},{12,8},{14,10},{16,20},{18,... | collective-permute-start | bytes 1769480 | tf_op jit(solution)/shard_map/ppermute | solution.py:42
  92.8 27.8 %collective-permute-start.35 = (bf16[192,1536]{1,0:T(8,128)(2,1)S(1)}, bf16[192,1536]{1,0:T(8,128)(2,1)S(1)}, u32[]{:S(2)}, u32[]{:S(2)}) collective-permute-start(bf16[192,1536]{1,0:T(8,128)(2,1)S(1)} %get-tuple-element.183), channel_id=1, source_target_pairs={{0,4},{2,6},{4,0},{6,2},{8,12},{10,14},{12,8},{14,10},{16,20},{18,... | collective-permute-start | bytes 1769480 | tf_op jit(solution)/shard_map/ppermute | solution.py:42
  95.5 34.8 %collective-permute-start.36 = (bf16[576,768]{1,0:T(8,128)(2,1)S(1)}, bf16[576,768]{1,0:T(8,128)(2,1)S(1)}, u32[]{:S(2)}, u32[]{:S(2)}) collective-permute-start(bf16[576,768]{1,0:T(8,128)(2,1)S(1)} %shard_map.291.own_ref), channel_id=1, source_target_pairs={{0,1},{1,0},{2,3},{3,2},{4,5},{5,4},{6,7},{7,6},{8,9},{9,8},{10,11... | collective-permute-start | bytes 2654216 | tf_op jit(solution)/shard_map/ppermute | solution.py:47
  106.5 14.1 %collective-permute-start.32 = (bf16[48,1536]{1,0:T(8,128)(2,1)S(1)}, bf16[48,1536]{1,0:T(8,128)(2,1)S(1)}, u32[]{:S(2)}, u32[]{:S(2)}) collective-permute-start(bf16[48,1536]{1,0:T(8,128)(2,1)S(1)} %get-tuple-element.176), channel_id=1, source_target_pairs={{0,8},{2,10},{4,12},{6,14},{8,0},{10,2},{12,4},{14,6},{16,24},{18,... | collective-permute-start | bytes 442376 | tf_op jit(solution)/shard_map/ppermute | solution.py:42
  106.6 14.1 %collective-permute-start.33 = (bf16[48,1536]{1,0:T(8,128)(2,1)S(1)}, bf16[48,1536]{1,0:T(8,128)(2,1)S(1)}, u32[]{:S(2)}, u32[]{:S(2)}) collective-permute-start(bf16[48,1536]{1,0:T(8,128)(2,1)S(1)} %get-tuple-element.177), channel_id=1, source_target_pairs={{0,16},{2,18},{4,20},{6,22},{8,24},{10,26},{12,28},{14,30},{16,0},... | collective-permute-start | bytes 442376 | tf_op jit(solution)/shard_map/ppermute | solution.py:42
  110.2 11.6 %collective-permute-start.34 = (bf16[48,1536]{1,0:T(8,128)(2,1)S(1)}, bf16[48,1536]{1,0:T(8,128)(2,1)S(1)}, u32[]{:S(2)}, u32[]{:S(2)}) collective-permute-start(bf16[48,1536]{1,0:T(8,128)(2,1)S(1)} %get-tuple-element.178), channel_id=1, source_target_pairs={{0,24},{2,26},{4,28},{6,30},{8,16},{10,18},{12,20},{14,22},{16,8},... | collective-permute-start | bytes 442376 | tf_op jit(solution)/shard_map/ppermute | solution.py:42
  123.8 14.9 %collective-permute-start.45 = (bf16[48,1536]{1,0:T(8,128)(2,1)S(1)}, bf16[48,1536]{1,0:T(8,128)(2,1)S(1)}, u32[]{:S(2)}, u32[]{:S(2)}) collective-permute-start(bf16[48,1536]{1,0:T(8,128)(2,1)S(1)} %get-tuple-element.199), channel_id=1, source_target_pairs={{0,8},{2,10},{4,12},{6,14},{8,0},{10,2},{12,4},{14,6},{16,24},{18,... | collective-permute-start | bytes 442376 | tf_op jit(solution)/shard_map/ppermute | solution.py:42
  123.9 14.9 %collective-permute-start.46 = (bf16[48,1536]{1,0:T(8,128)(2,1)S(1)}, bf16[48,1536]{1,0:T(8,128)(2,1)S(1)}, u32[]{:S(2)}, u32[]{:S(2)}) collective-permute-start(bf16[48,1536]{1,0:T(8,128)(2,1)S(1)} %get-tuple-element.200), channel_id=1, source_target_pairs={{0,16},{2,18},{4,20},{6,22},{8,24},{10,26},{12,28},{14,30},{16,0},... | collective-permute-start | bytes 442376 | tf_op jit(solution)/shard_map/ppermute | solution.py:42
  127.0 13.4 %collective-permute-start.47 = (bf16[48,1536]{1,0:T(8,128)(2,1)S(1)}, bf16[48,1536]{1,0:T(8,128)(2,1)S(1)}, u32[]{:S(2)}, u32[]{:S(2)}) collective-permute-start(bf16[48,1536]{1,0:T(8,128)(2,1)S(1)} %get-tuple-element.201), channel_id=1, source_target_pairs={{0,24},{2,26},{4,28},{6,30},{8,16},{10,18},{12,20},{14,22},{16,8},... | collective-permute-start | bytes 442376 | tf_op jit(solution)/shard_map/ppermute | solution.py:42
  128.7 15.4 %collective-permute-start.44 = (bf16[192,1536]{1,0:T(8,128)(2,1)S(1)}, bf16[192,1536]{1,0:T(8,128)(2,1)S(1)}, u32[]{:S(2)}, u32[]{:S(2)}) collective-permute-start(bf16[192,1536]{1,0:T(8,128)(2,1)S(1)} %get-tuple-element.196), channel_id=1, source_target_pairs={{0,4},{2,6},{4,0},{6,2},{8,12},{10,14},{12,8},{14,10},{16,20},{18,... | collective-permute-start | bytes 1769480 | tf_op jit(solution)/shard_map/ppermute | solution.py:42
  136.4 19.7 %collective-permute-start.39 = (bf16[576,768]{1,0:T(8,128)(2,1)S(1)}, bf16[576,768]{1,0:T(8,128)(2,1)S(1)}, u32[]{:S(2)}, u32[]{:S(2)}) collective-permute-start(bf16[576,768]{1,0:T(8,128)(2,1)S(1)} %get-tuple-element.204.own_ref), channel_id=1, source_target_pairs={{0,1},{1,0},{2,3},{3,2},{4,5},{5,4},{6,7},{7,6},{8,9},{9,8},{10,11... | collective-permute-start | bytes 2654216 | tf_op jit(solution)/shard_map/ppermute | solution.py:47
  144.2 15.9 %collective-permute-start.48 = (bf16[48,1664]{1,0:T(8,128)(2,1)S(1)}, bf16[48,1664]{1,0:T(8,128)(2,1)S(1)}, u32[]{:S(2)}, u32[]{:S(2)}) collective-permute-start(bf16[48,1664]{1,0:T(8,128)(2,1)S(1)} %get-tuple-element.216), channel_id=1, source_target_pairs={{0,8},{2,10},{4,12},{6,14},{8,0},{10,2},{12,4},{14,6},{16,24},{18,... | collective-permute-start | bytes 479240 | tf_op jit(solution)/shard_map/ppermute | solution.py:42
  145.6 14.5 %collective-permute-start.49 = (bf16[48,1664]{1,0:T(8,128)(2,1)S(1)}, bf16[48,1664]{1,0:T(8,128)(2,1)S(1)}, u32[]{:S(2)}, u32[]{:S(2)}) collective-permute-start(bf16[48,1664]{1,0:T(8,128)(2,1)S(1)} %get-tuple-element.217), channel_id=1, source_target_pairs={{0,16},{2,18},{4,20},{6,22},{8,24},{10,26},{12,28},{14,30},{16,0},... | collective-permute-start | bytes 479240 | tf_op jit(solution)/shard_map/ppermute | solution.py:42
  147.3 14.8 %collective-permute-start.50 = (bf16[48,1664]{1,0:T(8,128)(2,1)S(1)}, bf16[48,1664]{1,0:T(8,128)(2,1)S(1)}, u32[]{:S(2)}, u32[]{:S(2)}) collective-permute-start(bf16[48,1664]{1,0:T(8,128)(2,1)S(1)} %get-tuple-element.218), channel_id=1, source_target_pairs={{0,24},{2,26},{4,28},{6,30},{8,16},{10,18},{12,20},{14,22},{16,8},... | collective-permute-start | bytes 479240 | tf_op jit(solution)/shard_map/ppermute | solution.py:42
  (43 other events, 408.0 us)
where the time goes:
time: 164 us; the launch traced here: 163 us
  waiting for transfers between devices  59.5 us (36%)
  Pallas kernels  47.7 us (29%)
  starting transfers between devices  47.4 us (29%)
  local copies, waits for them, and re-layouts  4.75 us (3%)
  other arithmetic  2.33 us (1%)
    ppermute x45, waiting for transfers between devices, swap(): return lax.ppermute(array, 'dp', [(i, i ^ flip) for i in range(count)])  49.2 us
    pallas_call x21, Pallas kernels, call(): pl.pallas_call(kernel, out_shape=outs, in_specs=[SMEM] * scalars + [VMEM]...  46.2 us
    ppermute x45, starting transfers between devices, swap(): return lax.ppermute(array, 'dp', [(i, i ^ flip) for i in range(count)])  39.6 us
    ppermute x6, waiting for transfers between devices, swap_tensor(): return lax.ppermute(array, 'tensor', [(i, i ^ 1) for i in range(count)])  10.3 us
    ppermute x6, starting transfers between devices, swap_tensor(): return lax.ppermute(array, 'tensor', [(i, i ^ 1) for i in range(count)])  7.81 us
    unnamed x37, local copies, waits for them, and re-layouts  3.66 us
  transfers between devices with their start and end apart: 51, of which 22 were waited for; matrix products, arithmetic and copies ran while one was open for 2% of the time, Pallas kernels for 23%

commit v1 on v0

--- a/solution.py
+++ b/solution.py
@@ -108,7 +108,7 @@
 
 
 def by_rows(rows, body, carry=0):
-    step = next(size for size in (192, 144, 96, 48, rows) if rows % size == 0)
+    step = next(size for size in (288, 192, 144, 96, 48, rows) if rows % size == 0)
     return lax.fori_loop(0, rows // step, lambda i, c: body(pl.ds(pl.multiple_of(i * step, step), step), c), carry)
 
 

time: 164 us -> 163 us (level)
  Pallas kernels: 47.7 us -> 45.4 us
  waiting for transfers between devices: 59.5 us -> 61.5 us
    pallas_call x21, Pallas kernels: 46.2 us -> 43.8 us  [call(): pl.pallas_call(kernel, out_shape=outs, in_specs=[SMEM] * scalars + [VMEM]...]
    ppermute x45, waiting for transfers between devices: 49.2 us -> 51.4 us  [swap(): return lax.ppermute(array, 'dp', [(i, i ^ flip) for i in range(count)])]
  transfers between devices with their start and end apart: 51 -> 51, of which waited for: 22 -> 22; matrix products, arithmetic and copies ran while one was open for 2% -> 2% of each run, Pallas kernels for 23% -> 21%
where the time goes in v1:
time: 163 us
  waiting for transfers between devices  61.5 us (38%)
  starting transfers between devices  47.3 us (29%)
  Pallas kernels  45.4 us (28%)
  local copies, waits for them, and re-layouts  4.75 us (3%)
  other arithmetic  2.33 us (1%)
    ppermute x45, waiting for transfers between devices, swap(): return lax.ppermute(array, 'dp', [(i, i ^ flip) for i in range(count)])  51.4 us
    pallas_call x21, Pallas kernels, call(): pl.pallas_call(kernel, out_shape=outs, in_specs=[SMEM] * scalars + [VMEM]...  43.8 us
    ppermute x45, starting transfers between devices, swap(): return lax.ppermute(array, 'dp', [(i, i ^ flip) for i in range(count)])  39.6 us
    ppermute x6, waiting for transfers between devices, swap_tensor(): return lax.ppermute(array, 'tensor', [(i, i ^ 1) for i in range(count)])  10.1 us
    ppermute x6, starting transfers between devices, swap_tensor(): return lax.ppermute(array, 'tensor', [(i, i ^ 1) for i in range(count)])  7.75 us
    unnamed x37, local copies, waits for them, and re-layouts  3.66 us
  transfers between devices with their start and end apart: 51, of which 22 were waited for; matrix products, arithmetic and copies ran while one was open for 2% of the time, Pallas kernels for 21%

profile of v1, /device:TPU:8, one launch (start us, length us, event | category | flops | bytes accessed | tf_op | source)
XLA Modules:
  0.0 162.5 jit_solution(11017553720253099499)
XLA Ops:
  2.3 3.0 %collective-permute-start.2 = (bf16[48,1152]{1,0:T(8,128)(2,1)}, bf16[48,1152]{1,0:T(8,128)(2,1)S(1)}, u32[]{:S(2)}, u32[]{:S(2)}) collective-permute-start(bf16[48,1152]{1,0:T(8,128)(2,1)} %shard_map.280), channel_id=1, source_target_pairs={{0,16},{2,18},{4,20},{6,22},{8,24},{10,26},{12,28},{14,30},{16,0},... | collective-permute-start | bytes 331784 | tf_op jit(solution)/shard_map/ppermute | solution.py:42
  14.1 1.9 %shard_map.282 = (bf16[576,768]{1,0:T(8,128)(2,1)S(1)}, bf16[576,768]{1,0:T(8,128)(2,1)S(1)}) custom-call(s32[1,768]{1,0:T(1,128)S(1)} %add.53.order_ref, bf16[576,767]{1,0:T(8,128)(2,1)S(1)} %copy-done.1, bf16[768]{0:T(1024)(128)(2,1)S(1)} %copy-done.6), custom_call_target="tpu_custom_call" | custom-call | bytes 1024 | tf_op jit(solution)/shard_map/pallas_call | solution.py:71
  22.1 3.2 %collective-permute-done.7.refs_3_ = bf16[96,1152]{1,0:T(8,128)(2,1)S(1)} collective-permute-done((bf16[96,1152]{1,0:T(8,128)(2,1)S(1)}, bf16[96,1152]{1,0:T(8,128)(2,1)S(1)}, u32[]{:S(2)}, u32[]{:S(2)}) %collective-permute-start.7) | collective-permute-done | bytes 221216 | tf_op jit(solution)/shard_map/ppermute | solution.py:42
  25.2 3.5 %collective-permute-start.13 = (bf16[48,2304]{1,0:T(8,128)(2,1)S(1)}, bf16[48,2304]{1,0:T(8,128)(2,1)S(1)}, u32[]{:S(2)}, u32[]{:S(2)}) collective-permute-start(bf16[48,2304]{1,0:T(8,128)(2,1)S(1)} %shard_map.281), channel_id=1, source_target_pairs={{0,16},{2,18},{4,20},{6,22},{8,24},{10,26},{12,28},{14,30},{16,0},... | collective-permute-start | bytes 663560 | tf_op jit(solution)/shard_map/ppermute | solution.py:42
  31.3 5.9 %shard_map.283 = (bf16[576,1152]{1,0:T(8,128)(2,1)S(1)}, bf16[576,384]{1,0:T(8,128)(2,1)S(1)}, f32[8,576]{1,0:T(8,128)S(1)}) custom-call(s32[1,4]{1,0:T(1,128)S(1)} %copy-done.11, bf16[576,768]{1,0:T(8,128)(2,1)S(1)} %get-tuple-element.135.acts_ref.refs_2_.refs_4_, f32[1,1152]{1,0:T(1,128)S(1)} %fusion.1.bias_ref, ...), custom_call_target="tpu_custom_call" | custom-call | bytes 1024 | tf_op jit(solution)/shard_map/pallas_call | solution.py:71
  37.3 3.8 %collective-permute-done.13 = bf16[48,2304]{1,0:T(8,128)(2,1)S(1)} collective-permute-done((bf16[48,2304]{1,0:T(8,128)(2,1)S(1)}, bf16[48,2304]{1,0:T(8,128)(2,1)S(1)}, u32[]{:S(2)}, u32[]{:S(2)}) %collective-permute-start.13) | collective-permute-done | bytes 221216 | tf_op jit(solution)/shard_map/ppermute | solution.py:42
  41.0 3.3 %collective-permute-done.14 = bf16[48,2304]{1,0:T(8,128)(2,1)S(1)} collective-permute-done((bf16[48,2304]{1,0:T(8,128)(2,1)S(1)}, bf16[48,2304]{1,0:T(8,128)(2,1)S(1)}, u32[]{:S(2)}, u32[]{:S(2)}) %collective-permute-start.14) | collective-permute-done | bytes 221216 | tf_op jit(solution)/shard_map/ppermute | solution.py:42
  46.7 3.0 %collective-permute-start.18 = (bf16[96,1536]{1,0:T(8,128)(2,1)S(1)}, bf16[96,1536]{1,0:T(8,128)(2,1)S(1)}, u32[]{:S(2)}, u32[]{:S(2)}) collective-permute-start(bf16[96,1536]{1,0:T(8,128)(2,1)S(1)} %maximum_maximum_fusion.refs_4_.refs_1_), channel_id=1, source_target_pairs={{0,16},{2,18},{4,20},{6,22},{8,24},{10,26},{12,28},{14,30},{16,0},... | collective-permute-start | bytes 884744 | tf_op jit(solution)/shard_map/ppermute | solution.py:42
  50.2 3.2 %collective-permute-done.15.other_ref = bf16[576,384]{1,0:T(8,128)(2,1)S(1)} collective-permute-done((bf16[576,384]{1,0:T(8,128)(2,1)S(1)}, bf16[576,384]{1,0:T(8,128)(2,1)S(1)}, u32[]{:S(2)}, u32[]{:S(2)}) %collective-permute-start.15) | collective-permute-done | bytes 442400 | tf_op jit(solution)/shard_map/ppermute | solution.py:47
  56.6 10.5 %collective-permute-done.18.refs_6_.refs_3_ = bf16[96,1536]{1,0:T(8,128)(2,1)S(1)} collective-permute-done((bf16[96,1536]{1,0:T(8,128)(2,1)S(1)}, bf16[96,1536]{1,0:T(8,128)(2,1)S(1)}, u32[]{:S(2)}, u32[]{:S(2)}) %collective-permute-start.18) | collective-permute-done | bytes 294944 | tf_op jit(solution)/shard_map/ppermute | solution.py:42
  67.1 4.5 %collective-permute-done.19.refs_7_.refs_4_ = bf16[96,1536]{1,0:T(8,128)(2,1)S(1)} collective-permute-done((bf16[96,1536]{1,0:T(8,128)(2,1)S(1)}, bf16[96,1536]{1,0:T(8,128)(2,1)S(1)}, u32[]{:S(2)}, u32[]{:S(2)}) %collective-permute-start.19) | collective-permute-done | bytes 294944 | tf_op jit(solution)/shard_map/ppermute | solution.py:42
  72.7 3.1 %collective-permute-done.22.refs_8_.refs_5_ = bf16[96,1536]{1,0:T(8,128)(2,1)S(1)} collective-permute-done((bf16[96,1536]{1,0:T(8,128)(2,1)S(1)}, bf16[96,1536]{1,0:T(8,128)(2,1)S(1)}, u32[]{:S(2)}, u32[]{:S(2)}) %collective-permute-start.22) | collective-permute-done | bytes 294944 | tf_op jit(solution)/shard_map/ppermute | solution.py:42
  77.4 7.3 %shard_map.285 = (f32[576,768]{1,0:T(8,128)S(1)}, bf16[576,768]{1,0:T(8,128)(2,1)S(1)}, bf16[576,1536]{1,0:T(8,128)(2,1)S(1)}, bf16[576,1536]{1,0:T(8,128)(2,1)S...) custom-call(s32[1,1]{1,0:T(1,128)} %bitcast.2.rank_ref, s32[1,768]{1,0:T(1,128)S(1)} %add.53.order_ref, ...), custom_call_target="tpu_custom_call" | custom-call | bytes 1024 | tf_op jit(solution)/shard_map/pallas_call | solution.py:71
  96.6 9.4 %collective-permute-done.29.refs_1_ = bf16[192,1536]{1,0:T(8,128)(2,1)S(1)} collective-permute-done((bf16[192,1536]{1,0:T(8,128)(2,1)S(1)}, bf16[192,1536]{1,0:T(8,128)(2,1)S(1)}, u32[]{:S(2)}, u32[]{:S(2)}) %collective-permute-start.29) | collective-permute-done | bytes 589856 | tf_op jit(solution)/shard_map/ppermute | solution.py:42
  106.2 3.7 %collective-permute-start.33 = (bf16[48,1536]{1,0:T(8,128)(2,1)S(1)}, bf16[48,1536]{1,0:T(8,128)(2,1)S(1)}, u32[]{:S(2)}, u32[]{:S(2)}) collective-permute-start(bf16[48,1536]{1,0:T(8,128)(2,1)S(1)} %get-tuple-element.177), channel_id=1, source_target_pairs={{0,16},{2,18},{4,20},{6,22},{8,24},{10,26},{12,28},{14,30},{16,0},... | collective-permute-start | bytes 442376 | tf_op jit(solution)/shard_map/ppermute | solution.py:42
  111.0 2.7 %shard_map.292 = (f32[576,768]{1,0:T(8,128)S(1)}, bf16[576,768]{1,0:T(8,128)(2,1)S(1)}, bf16[576,384]{1,0:T(8,128)(2,1)S(1)}, f32[8,768]{1,0:T(8,128)S(1)}) custom-call(s32[1,768]{1,0:T(1,128)S(1)} %add.53.order_ref, f32[8,768]{1,0:T(8,128)S(1)} %get-tuple-element.160.row_ref, bf16[576,768]{1,0:T(8,128)(2,1)S(1)} %get-tuple-element.170.own_ref, ...), custom_call_target="tpu_custom_call" | custom-call | bytes 1024 | tf_op jit(solution)/shard_map/pallas_call | solution.py:71
  113.7 6.2 %shard_map.293 = (bf16[576,384]{1,0:T(8,128)(2,1)S(1)}, bf16[576,768]{1,0:T(8,128)(2,1)S(1)}) custom-call(s32[1,4]{1,0:T(1,128)S(1)} %copy-done.11, bf16[576,1152]{1,0:T(8,128)(2,1)S(1)} %get-tuple-element.140.qkv_ref, f32[8,576]{1,0:T(8,128)S(1)} %get-tuple-element.141.lse_ref, bf16[576,384]{1,0:T(8,128)(2,1)S(1)} %get-tuple-element.188.refs_0_), custom_call_target="tpu_custom_call" | custom-call | flops 99999997952 | bytes 1024 | tf_op jit(solution)/shard_map/pallas_call | solution.py:71
  123.5 3.1 %collective-permute-start.46 = (bf16[48,1536]{1,0:T(8,128)(2,1)S(1)}, bf16[48,1536]{1,0:T(8,128)(2,1)S(1)}, u32[]{:S(2)}, u32[]{:S(2)}) collective-permute-start(bf16[48,1536]{1,0:T(8,128)(2,1)S(1)} %get-tuple-element.200), channel_id=1, source_target_pairs={{0,16},{2,18},{4,20},{6,22},{8,24},{10,26},{12,28},{14,30},{16,0},... | collective-permute-start | bytes 442376 | tf_op jit(solution)/shard_map/ppermute | solution.py:42
  133.0 2.3 %collective-permute-done.40.gain_other = f32[1,768]{1,0:T(1,128)S(1)} collective-permute-done((f32[1,768]{1,0:T(1,128)S(1)}, f32[1,768]{1,0:T(1,128)S(1)}, u32[]{:S(2)}, u32[]{:S(2)}) %collective-permute-start.40) | collective-permute-done | bytes 3104 | tf_op jit(solution)/shard_map/ppermute | solution.py:47
  140.9 2.8 %collective-permute-done.42 = f32[48,128]{1,0:T(8,128)S(1)} collective-permute-done((f32[48,128]{1,0:T(8,128)S(1)}, f32[48,128]{1,0:T(8,128)S(1)}, u32[]{:S(2)}, u32[]{:S(2)}) %collective-permute-start.42) | collective-permute-done | bytes 24608 | tf_op jit(solution)/shard_map/ppermute | solution.py:42
  148.2 2.5 %shard_map.300 = bf16[576,767]{1,0:T(8,128)(2,1)} custom-call(s32[1,768]{1,0:T(1,128)S(1)} %add.53.order_ref, f32[8,768]{1,0:T(8,128)S(1)} %copy-done.3, f32[576,768]{1,0:T(8,128)S(1)} %get-tuple-element.186.mid_ref, bf16[576,768]{1,0:T(8,128)(2,1)S(1)} %shard_map.291.own_ref, bf16[576,768]{1,0:T(8,128)(2,1)S(1)} %collective-permute-done.36.other_ref), custom_call_target="tpu_custom_call" | custom-call | bytes 1024 | tf_op jit(solution)/shard_map/pallas_call | solution.py:71
  150.6 4.4 %collective-permute-done.39.other_ref = bf16[576,768]{1,0:T(8,128)(2,1)S(1)} collective-permute-done((bf16[576,768]{1,0:T(8,128)(2,1)S(1)}, bf16[576,768]{1,0:T(8,128)(2,1)S(1)}, u32[]{:S(2)}, u32[]{:S(2)}) %collective-permute-start.39) | collective-permute-done | bytes 884768 | tf_op jit(solution)/shard_map/ppermute | solution.py:47
  155.1 3.4 %shard_map.301 = bf16[576,767]{1,0:T(8,128)(2,1)} custom-call(s32[1,768]{1,0:T(1,128)S(1)} %add.53.order_ref, f32[8,768]{1,0:T(8,128)S(1)} %copy-done.3, bf16[576,768]{1,0:T(8,128)(2,1)S(1)} %get-tuple-element.204.own_ref, bf16[576,768]{1,0:T(8,128)(2,1)S(1)} %collective-permute-done.39.other_ref, bf16[576,768]{1,0:T(8,128)(2,1)S(1)} %get-tuple-element.146.ent_in.ent_ref, ...), custom_call_target="tpu_custom_call" | custom-call | bytes 1024 | tf_op jit(solution)/shard_map/pallas_call | solution.py:71
  158.5 3.3 %collective-permute-done.50.refs_2_ = bf16[48,1664]{1,0:T(8,128)(2,1)S(1)} collective-permute-done((bf16[48,1664]{1,0:T(8,128)(2,1)S(1)}, bf16[48,1664]{1,0:T(8,128)(2,1)S(1)}, u32[]{:S(2)}, u32[]{:S(2)}) %collective-permute-start.50) | collective-permute-done | bytes 159776 | tf_op jit(solution)/shard_map/ppermute | solution.py:42
  (155 shorter events, 61.5 us)
Async XLA Ops:
  2.2 15.6 %collective-permute-start.1 = (bf16[48,1152]{1,0:T(8,128)(2,1)}, bf16[48,1152]{1,0:T(8,128)(2,1)S(1)}, u32[]{:S(2)}, u32[]{:S(2)}) collective-permute-start(bf16[48,1152]{1,0:T(8,128)(2,1)} %shard_map.280), channel_id=1, source_target_pairs={{0,8},{2,10},{4,12},{6,14},{8,0},{10,2},{12,4},{14,6},{16,24},{18,... | collective-permute-start | bytes 331784 | tf_op jit(solution)/shard_map/ppermute | solution.py:42
  2.3 15.6 %collective-permute-start.2 = (bf16[48,1152]{1,0:T(8,128)(2,1)}, bf16[48,1152]{1,0:T(8,128)(2,1)S(1)}, u32[]{:S(2)}, u32[]{:S(2)}) collective-permute-start(bf16[48,1152]{1,0:T(8,128)(2,1)} %shard_map.280), channel_id=1, source_target_pairs={{0,16},{2,18},{4,20},{6,22},{8,24},{10,26},{12,28},{14,30},{16,0},... | collective-permute-start | bytes 331784 | tf_op jit(solution)/shard_map/ppermute | solution.py:42
  5.3 12.5 %collective-permute-start.3 = (bf16[48,1152]{1,0:T(8,128)(2,1)}, bf16[48,1152]{1,0:T(8,128)(2,1)S(1)}, u32[]{:S(2)}, u32[]{:S(2)}) collective-permute-start(bf16[48,1152]{1,0:T(8,128)(2,1)} %shard_map.280), channel_id=1, source_target_pairs={{0,24},{2,26},{4,28},{6,30},{8,16},{10,18},{12,20},{14,22},{16,8},... | collective-permute-start | bytes 331784 | tf_op jit(solution)/shard_map/ppermute | solution.py:42
  20.6 16.6 %collective-permute-start.12 = (bf16[48,2304]{1,0:T(8,128)(2,1)S(1)}, bf16[48,2304]{1,0:T(8,128)(2,1)S(1)}, u32[]{:S(2)}, u32[]{:S(2)}) collective-permute-start(bf16[48,2304]{1,0:T(8,128)(2,1)S(1)} %shard_map.281), channel_id=1, source_target_pairs={{0,8},{2,10},{4,12},{6,14},{8,0},{10,2},{12,4},{14,6},{16,24},{18,... | collective-permute-start | bytes 663560 | tf_op jit(solution)/shard_map/ppermute | solution.py:42
  25.2 15.8 %collective-permute-start.13 = (bf16[48,2304]{1,0:T(8,128)(2,1)S(1)}, bf16[48,2304]{1,0:T(8,128)(2,1)S(1)}, u32[]{:S(2)}, u32[]{:S(2)}) collective-permute-start(bf16[48,2304]{1,0:T(8,128)(2,1)S(1)} %shard_map.281), channel_id=1, source_target_pairs={{0,16},{2,18},{4,20},{6,22},{8,24},{10,26},{12,28},{14,30},{16,0},... | collective-permute-start | bytes 663560 | tf_op jit(solution)/shard_map/ppermute | solution.py:42
  28.7 15.6 %collective-permute-start.14 = (bf16[48,2304]{1,0:T(8,128)(2,1)S(1)}, bf16[48,2304]{1,0:T(8,128)(2,1)S(1)}, u32[]{:S(2)}, u32[]{:S(2)}) collective-permute-start(bf16[48,2304]{1,0:T(8,128)(2,1)S(1)} %shard_map.281), channel_id=1, source_target_pairs={{0,24},{2,26},{4,28},{6,30},{8,16},{10,18},{12,20},{14,22},{16,8},... | collective-permute-start | bytes 663560 | tf_op jit(solution)/shard_map/ppermute | solution.py:42
  44.5 27.2 %collective-permute-start.16 = (bf16[192,2304]{1,0:T(8,128)(2,1)S(1)}, bf16[192,2304]{1,0:T(8,128)(2,1)S(1)}, u32[]{:S(2)}, u32[]{:S(2)}) collective-permute-start(bf16[192,2304]{1,0:T(8,128)(2,1)S(1)} %constant_dynamic-update-slice_fusion.4.refs_0_), channel_id=1, source_target_pairs={{0,4},{2,6},{4,0},{6,2},{8,12},{10,14},{12,8},{14,10},{16,20},{18,... | collective-permute-start | bytes 2654216 | tf_op jit(solution)/shard_map/ppermute | solution.py:42
  46.7 20.4 %collective-permute-start.18 = (bf16[96,1536]{1,0:T(8,128)(2,1)S(1)}, bf16[96,1536]{1,0:T(8,128)(2,1)S(1)}, u32[]{:S(2)}, u32[]{:S(2)}) collective-permute-start(bf16[96,1536]{1,0:T(8,128)(2,1)S(1)} %maximum_maximum_fusion.refs_4_.refs_1_), channel_id=1, source_target_pairs={{0,16},{2,18},{4,20},{6,22},{8,24},{10,26},{12,28},{14,30},{16,0},... | collective-permute-start | bytes 884744 | tf_op jit(solution)/shard_map/ppermute | solution.py:42
  49.7 22.0 %collective-permute-start.19 = (bf16[96,1536]{1,0:T(8,128)(2,1)S(1)}, bf16[96,1536]{1,0:T(8,128)(2,1)S(1)}, u32[]{:S(2)}, u32[]{:S(2)}) collective-permute-start(bf16[96,1536]{1,0:T(8,128)(2,1)S(1)} %maximum_maximum_fusion.refs_4_.refs_1_), channel_id=1, source_target_pairs={{0,24},{2,26},{4,28},{6,30},{8,16},{10,18},{12,20},{14,22},{16,8},... | collective-permute-start | bytes 884744 | tf_op jit(solution)/shard_map/ppermute | solution.py:42
  86.3 23.5 %collective-permute-start.26 = (bf16[576,768]{1,0:T(8,128)(2,1)S(1)}, bf16[576,768]{1,0:T(8,128)(2,1)S(1)}, u32[]{:S(2)}, u32[]{:S(2)}) collective-permute-start(bf16[576,768]{1,0:T(8,128)(2,1)S(1)} %get-tuple-element.170.own_ref), channel_id=1, source_target_pairs={{0,1},{1,0},{2,3},{3,2},{4,5},{5,4},{6,7},{7,6},{8,9},{9,8},{10,11... | collective-permute-start | bytes 2654216 | tf_op jit(solution)/shard_map/ppermute | solution.py:47
  89.7 16.2 %collective-permute-start.29 = (bf16[192,1536]{1,0:T(8,128)(2,1)S(1)}, bf16[192,1536]{1,0:T(8,128)(2,1)S(1)}, u32[]{:S(2)}, u32[]{:S(2)}) collective-permute-start(bf16[192,1536]{1,0:T(8,128)(2,1)S(1)} %get-tuple-element.175), channel_id=1, source_target_pairs={{0,4},{2,6},{4,0},{6,2},{8,12},{10,14},{12,8},{14,10},{16,20},{18,... | collective-permute-start | bytes 1769480 | tf_op jit(solution)/shard_map/ppermute | solution.py:42
  92.4 27.5 %collective-permute-start.35 = (bf16[192,1536]{1,0:T(8,128)(2,1)S(1)}, bf16[192,1536]{1,0:T(8,128)(2,1)S(1)}, u32[]{:S(2)}, u32[]{:S(2)}) collective-permute-start(bf16[192,1536]{1,0:T(8,128)(2,1)S(1)} %get-tuple-element.183), channel_id=1, source_target_pairs={{0,4},{2,6},{4,0},{6,2},{8,12},{10,14},{12,8},{14,10},{16,20},{18,... | collective-permute-start | bytes 1769480 | tf_op jit(solution)/shard_map/ppermute | solution.py:42
  95.1 34.8 %collective-permute-start.36 = (bf16[576,768]{1,0:T(8,128)(2,1)S(1)}, bf16[576,768]{1,0:T(8,128)(2,1)S(1)}, u32[]{:S(2)}, u32[]{:S(2)}) collective-permute-start(bf16[576,768]{1,0:T(8,128)(2,1)S(1)} %shard_map.291.own_ref), channel_id=1, source_target_pairs={{0,1},{1,0},{2,3},{3,2},{4,5},{5,4},{6,7},{7,6},{8,9},{9,8},{10,11... | collective-permute-start | bytes 2654216 | tf_op jit(solution)/shard_map/ppermute | solution.py:47
  106.1 13.8 %collective-permute-start.32 = (bf16[48,1536]{1,0:T(8,128)(2,1)S(1)}, bf16[48,1536]{1,0:T(8,128)(2,1)S(1)}, u32[]{:S(2)}, u32[]{:S(2)}) collective-permute-start(bf16[48,1536]{1,0:T(8,128)(2,1)S(1)} %get-tuple-element.176), channel_id=1, source_target_pairs={{0,8},{2,10},{4,12},{6,14},{8,0},{10,2},{12,4},{14,6},{16,24},{18,... | collective-permute-start | bytes 442376 | tf_op jit(solution)/shard_map/ppermute | solution.py:42
  106.2 13.8 %collective-permute-start.33 = (bf16[48,1536]{1,0:T(8,128)(2,1)S(1)}, bf16[48,1536]{1,0:T(8,128)(2,1)S(1)}, u32[]{:S(2)}, u32[]{:S(2)}) collective-permute-start(bf16[48,1536]{1,0:T(8,128)(2,1)S(1)} %get-tuple-element.177), channel_id=1, source_target_pairs={{0,16},{2,18},{4,20},{6,22},{8,24},{10,26},{12,28},{14,30},{16,0},... | collective-permute-start | bytes 442376 | tf_op jit(solution)/shard_map/ppermute | solution.py:42
  109.9 11.6 %collective-permute-start.34 = (bf16[48,1536]{1,0:T(8,128)(2,1)S(1)}, bf16[48,1536]{1,0:T(8,128)(2,1)S(1)}, u32[]{:S(2)}, u32[]{:S(2)}) collective-permute-start(bf16[48,1536]{1,0:T(8,128)(2,1)S(1)} %get-tuple-element.178), channel_id=1, source_target_pairs={{0,24},{2,26},{4,28},{6,30},{8,16},{10,18},{12,20},{14,22},{16,8},... | collective-permute-start | bytes 442376 | tf_op jit(solution)/shard_map/ppermute | solution.py:42
  123.4 14.2 %collective-permute-start.45 = (bf16[48,1536]{1,0:T(8,128)(2,1)S(1)}, bf16[48,1536]{1,0:T(8,128)(2,1)S(1)}, u32[]{:S(2)}, u32[]{:S(2)}) collective-permute-start(bf16[48,1536]{1,0:T(8,128)(2,1)S(1)} %get-tuple-element.199), channel_id=1, source_target_pairs={{0,8},{2,10},{4,12},{6,14},{8,0},{10,2},{12,4},{14,6},{16,24},{18,... | collective-permute-start | bytes 442376 | tf_op jit(solution)/shard_map/ppermute | solution.py:42
  123.5 14.2 %collective-permute-start.46 = (bf16[48,1536]{1,0:T(8,128)(2,1)S(1)}, bf16[48,1536]{1,0:T(8,128)(2,1)S(1)}, u32[]{:S(2)}, u32[]{:S(2)}) collective-permute-start(bf16[48,1536]{1,0:T(8,128)(2,1)S(1)} %get-tuple-element.200), channel_id=1, source_target_pairs={{0,16},{2,18},{4,20},{6,22},{8,24},{10,26},{12,28},{14,30},{16,0},... | collective-permute-start | bytes 442376 | tf_op jit(solution)/shard_map/ppermute | solution.py:42
  126.6 13.4 %collective-permute-start.47 = (bf16[48,1536]{1,0:T(8,128)(2,1)S(1)}, bf16[48,1536]{1,0:T(8,128)(2,1)S(1)}, u32[]{:S(2)}, u32[]{:S(2)}) collective-permute-start(bf16[48,1536]{1,0:T(8,128)(2,1)S(1)} %get-tuple-element.201), channel_id=1, source_target_pairs={{0,24},{2,26},{4,28},{6,30},{8,16},{10,18},{12,20},{14,22},{16,8},... | collective-permute-start | bytes 442376 | tf_op jit(solution)/shard_map/ppermute | solution.py:42
  128.3 15.4 %collective-permute-start.44 = (bf16[192,1536]{1,0:T(8,128)(2,1)S(1)}, bf16[192,1536]{1,0:T(8,128)(2,1)S(1)}, u32[]{:S(2)}, u32[]{:S(2)}) collective-permute-start(bf16[192,1536]{1,0:T(8,128)(2,1)S(1)} %get-tuple-element.196), channel_id=1, source_target_pairs={{0,4},{2,6},{4,0},{6,2},{8,12},{10,14},{12,8},{14,10},{16,20},{18,... | collective-permute-start | bytes 1769480 | tf_op jit(solution)/shard_map/ppermute | solution.py:42
  135.3 19.7 %collective-permute-start.39 = (bf16[576,768]{1,0:T(8,128)(2,1)S(1)}, bf16[576,768]{1,0:T(8,128)(2,1)S(1)}, u32[]{:S(2)}, u32[]{:S(2)}) collective-permute-start(bf16[576,768]{1,0:T(8,128)(2,1)S(1)} %get-tuple-element.204.own_ref), channel_id=1, source_target_pairs={{0,1},{1,0},{2,3},{3,2},{4,5},{5,4},{6,7},{7,6},{8,9},{9,8},{10,11... | collective-permute-start | bytes 2654216 | tf_op jit(solution)/shard_map/ppermute | solution.py:47
  143.8 14.7 %collective-permute-start.48 = (bf16[48,1664]{1,0:T(8,128)(2,1)S(1)}, bf16[48,1664]{1,0:T(8,128)(2,1)S(1)}, u32[]{:S(2)}, u32[]{:S(2)}) collective-permute-start(bf16[48,1664]{1,0:T(8,128)(2,1)S(1)} %get-tuple-element.216), channel_id=1, source_target_pairs={{0,8},{2,10},{4,12},{6,14},{8,0},{10,2},{12,4},{14,6},{16,24},{18,... | collective-permute-start | bytes 479240 | tf_op jit(solution)/shard_map/ppermute | solution.py:42
  145.2 13.3 %collective-permute-start.49 = (bf16[48,1664]{1,0:T(8,128)(2,1)S(1)}, bf16[48,1664]{1,0:T(8,128)(2,1)S(1)}, u32[]{:S(2)}, u32[]{:S(2)}) collective-permute-start(bf16[48,1664]{1,0:T(8,128)(2,1)S(1)} %get-tuple-element.217), channel_id=1, source_target_pairs={{0,16},{2,18},{4,20},{6,22},{8,24},{10,26},{12,28},{14,30},{16,0},... | collective-permute-start | bytes 479240 | tf_op jit(solution)/shard_map/ppermute | solution.py:42
  146.9 14.8 %collective-permute-start.50 = (bf16[48,1664]{1,0:T(8,128)(2,1)S(1)}, bf16[48,1664]{1,0:T(8,128)(2,1)S(1)}, u32[]{:S(2)}, u32[]{:S(2)}) collective-permute-start(bf16[48,1664]{1,0:T(8,128)(2,1)S(1)} %get-tuple-element.218), channel_id=1, source_target_pairs={{0,24},{2,26},{4,28},{6,30},{8,16},{10,18},{12,20},{14,22},{16,8},... | collective-permute-start | bytes 479240 | tf_op jit(solution)/shard_map/ppermute | solution.py:42
  (43 other events, 406.1 us)

commit v2 on v1

--- a/solution.py
+++ b/solution.py
@@ -105,6 +105,10 @@
 
 def center(rows):
     return rows - jnp.mean(rows, axis=1, keepdims=True)
+
+
+def by_rows_one(rows, body, carry=0):
+    return body(slice(0, rows), carry)
 
 
 def by_rows(rows, body, carry=0):
@@ -174,7 +178,7 @@
         acts_ref[at, :] = (normed * gain).astype(BF16)
         return carry
 
-    by_rows(stream_ref.shape[0], one)
+    by_rows_one(stream_ref.shape[0], one)
 
 
 def prepare_kernel(rank_ref, order_ref, cot_ref, own_ref, other_ref, ent_in, *refs):
@@ -327,7 +331,7 @@
         )
 
     zero = jnp.zeros((1, sum_ref.shape[1]), F32)
-    sum_ref[0:1, :], sum_ref[1:2, :] = by_rows(own_ref.shape[0], one, (zero, zero))
+    sum_ref[0:1, :], sum_ref[1:2, :] = by_rows_one(own_ref.shape[0], one, (zero, zero))
     sum_ref[2:, :] = jnp.zeros((sum_ref.shape[0] - 2, sum_ref.shape[1]), F32)
 
 

time: 163 us -> 163 us (level)
  no operation moved by 1% of the time
where the time goes in v2:
time: 163 us; the launch traced here: 162 us
  waiting for transfers between devices  61.8 us (38%)
  starting transfers between devices  47.4 us (29%)
  Pallas kernels  44.8 us (27%)
  local copies, waits for them, and re-layouts  4.75 us (3%)
  other arithmetic  2.33 us (1%)
    ppermute x45, waiting for transfers between devices, swap(): return lax.ppermute(array, 'dp', [(i, i ^ flip) for i in range(count)])  51.6 us
    pallas_call x21, Pallas kernels, call(): pl.pallas_call(kernel, out_shape=outs, in_specs=[SMEM] * scalars + [VMEM]...  43.2 us
    ppermute x45, starting transfers between devices, swap(): return lax.ppermute(array, 'dp', [(i, i ^ flip) for i in range(count)])  39.7 us
    ppermute x6, waiting for transfers between devices, swap_tensor(): return lax.ppermute(array, 'tensor', [(i, i ^ 1) for i in range(count)])  10.2 us
    ppermute x6, starting transfers between devices, swap_tensor(): return lax.ppermute(array, 'tensor', [(i, i ^ 1) for i in range(count)])  7.69 us
    unnamed x37, local copies, waits for them, and re-layouts  3.66 us
  transfers between devices with their start and end apart: 51, of which 22 were waited for; matrix products, arithmetic and copies ran while one was open for 2% of the time, Pallas kernels for 21%

profile of v2, /device:TPU:8, one launch (start us, length us, event | category | flops | bytes accessed | tf_op | source)
XLA Modules:
  0.0 162.2 jit_solution(9606826092694878041)
XLA Ops:
  2.3 3.0 %collective-permute-start.2 = (bf16[48,1152]{1,0:T(8,128)(2,1)}, bf16[48,1152]{1,0:T(8,128)(2,1)S(1)}, u32[]{:S(2)}, u32[]{:S(2)}) collective-permute-start(bf16[48,1152]{1,0:T(8,128)(2,1)} %shard_map.280), channel_id=1, source_target_pairs={{0,16},{2,18},{4,20},{6,22},{8,24},{10,26},{12,28},{14,30},{16,0},... | collective-permute-start | bytes 331784 | tf_op jit(solution)/shard_map/ppermute | solution.py:42
  21.7 3.2 %collective-permute-done.7.refs_3_ = bf16[96,1152]{1,0:T(8,128)(2,1)S(1)} collective-permute-done((bf16[96,1152]{1,0:T(8,128)(2,1)S(1)}, bf16[96,1152]{1,0:T(8,128)(2,1)S(1)}, u32[]{:S(2)}, u32[]{:S(2)}) %collective-permute-start.7) | collective-permute-done | bytes 221216 | tf_op jit(solution)/shard_map/ppermute | solution.py:42
  24.9 3.5 %collective-permute-start.13 = (bf16[48,2304]{1,0:T(8,128)(2,1)S(1)}, bf16[48,2304]{1,0:T(8,128)(2,1)S(1)}, u32[]{:S(2)}, u32[]{:S(2)}) collective-permute-start(bf16[48,2304]{1,0:T(8,128)(2,1)S(1)} %shard_map.281), channel_id=1, source_target_pairs={{0,16},{2,18},{4,20},{6,22},{8,24},{10,26},{12,28},{14,30},{16,0},... | collective-permute-start | bytes 663560 | tf_op jit(solution)/shard_map/ppermute | solution.py:42
  30.9 5.9 %shard_map.283 = (bf16[576,1152]{1,0:T(8,128)(2,1)S(1)}, bf16[576,384]{1,0:T(8,128)(2,1)S(1)}, f32[8,576]{1,0:T(8,128)S(1)}) custom-call(s32[1,4]{1,0:T(1,128)S(1)} %copy-done.11, bf16[576,768]{1,0:T(8,128)(2,1)S(1)} %get-tuple-element.135.acts_ref.refs_2_.refs_4_, f32[1,1152]{1,0:T(1,128)S(1)} %fusion.1.bias_ref, ...), custom_call_target="tpu_custom_call" | custom-call | bytes 1024 | tf_op jit(solution)/shard_map/pallas_call | solution.py:71
  36.9 3.8 %collective-permute-done.13 = bf16[48,2304]{1,0:T(8,128)(2,1)S(1)} collective-permute-done((bf16[48,2304]{1,0:T(8,128)(2,1)S(1)}, bf16[48,2304]{1,0:T(8,128)(2,1)S(1)}, u32[]{:S(2)}, u32[]{:S(2)}) %collective-permute-start.13) | collective-permute-done | bytes 221216 | tf_op jit(solution)/shard_map/ppermute | solution.py:42
  40.7 3.3 %collective-permute-done.14 = bf16[48,2304]{1,0:T(8,128)(2,1)S(1)} collective-permute-done((bf16[48,2304]{1,0:T(8,128)(2,1)S(1)}, bf16[48,2304]{1,0:T(8,128)(2,1)S(1)}, u32[]{:S(2)}, u32[]{:S(2)}) %collective-permute-start.14) | collective-permute-done | bytes 221216 | tf_op jit(solution)/shard_map/ppermute | solution.py:42
  46.3 3.0 %collective-permute-start.18 = (bf16[96,1536]{1,0:T(8,128)(2,1)S(1)}, bf16[96,1536]{1,0:T(8,128)(2,1)S(1)}, u32[]{:S(2)}, u32[]{:S(2)}) collective-permute-start(bf16[96,1536]{1,0:T(8,128)(2,1)S(1)} %maximum_maximum_fusion.refs_4_.refs_1_), channel_id=1, source_target_pairs={{0,16},{2,18},{4,20},{6,22},{8,24},{10,26},{12,28},{14,30},{16,0},... | collective-permute-start | bytes 884744 | tf_op jit(solution)/shard_map/ppermute | solution.py:42
  49.8 3.2 %collective-permute-done.15.other_ref = bf16[576,384]{1,0:T(8,128)(2,1)S(1)} collective-permute-done((bf16[576,384]{1,0:T(8,128)(2,1)S(1)}, bf16[576,384]{1,0:T(8,128)(2,1)S(1)}, u32[]{:S(2)}, u32[]{:S(2)}) %collective-permute-start.15) | collective-permute-done | bytes 442400 | tf_op jit(solution)/shard_map/ppermute | solution.py:47
  56.3 10.5 %collective-permute-done.18.refs_6_.refs_3_ = bf16[96,1536]{1,0:T(8,128)(2,1)S(1)} collective-permute-done((bf16[96,1536]{1,0:T(8,128)(2,1)S(1)}, bf16[96,1536]{1,0:T(8,128)(2,1)S(1)}, u32[]{:S(2)}, u32[]{:S(2)}) %collective-permute-start.18) | collective-permute-done | bytes 294944 | tf_op jit(solution)/shard_map/ppermute | solution.py:42
  66.8 4.5 %collective-permute-done.19.refs_7_.refs_4_ = bf16[96,1536]{1,0:T(8,128)(2,1)S(1)} collective-permute-done((bf16[96,1536]{1,0:T(8,128)(2,1)S(1)}, bf16[96,1536]{1,0:T(8,128)(2,1)S(1)}, u32[]{:S(2)}, u32[]{:S(2)}) %collective-permute-start.19) | collective-permute-done | bytes 294944 | tf_op jit(solution)/shard_map/ppermute | solution.py:42
  72.3 3.1 %collective-permute-done.22.refs_8_.refs_5_ = bf16[96,1536]{1,0:T(8,128)(2,1)S(1)} collective-permute-done((bf16[96,1536]{1,0:T(8,128)(2,1)S(1)}, bf16[96,1536]{1,0:T(8,128)(2,1)S(1)}, u32[]{:S(2)}, u32[]{:S(2)}) %collective-permute-start.22) | collective-permute-done | bytes 294944 | tf_op jit(solution)/shard_map/ppermute | solution.py:42
  77.0 7.3 %shard_map.285 = (f32[576,768]{1,0:T(8,128)S(1)}, bf16[576,768]{1,0:T(8,128)(2,1)S(1)}, bf16[576,1536]{1,0:T(8,128)(2,1)S(1)}, bf16[576,1536]{1,0:T(8,128)(2,1)S...) custom-call(s32[1,1]{1,0:T(1,128)} %bitcast.2.rank_ref, s32[1,768]{1,0:T(1,128)S(1)} %add.53.order_ref, ...), custom_call_target="tpu_custom_call" | custom-call | bytes 1024 | tf_op jit(solution)/shard_map/pallas_call | solution.py:71
  96.3 9.3 %collective-permute-done.29.refs_1_ = bf16[192,1536]{1,0:T(8,128)(2,1)S(1)} collective-permute-done((bf16[192,1536]{1,0:T(8,128)(2,1)S(1)}, bf16[192,1536]{1,0:T(8,128)(2,1)S(1)}, u32[]{:S(2)}, u32[]{:S(2)}) %collective-permute-start.29) | collective-permute-done | bytes 589856 | tf_op jit(solution)/shard_map/ppermute | solution.py:42
  105.8 3.7 %collective-permute-start.33 = (bf16[48,1536]{1,0:T(8,128)(2,1)S(1)}, bf16[48,1536]{1,0:T(8,128)(2,1)S(1)}, u32[]{:S(2)}, u32[]{:S(2)}) collective-permute-start(bf16[48,1536]{1,0:T(8,128)(2,1)S(1)} %get-tuple-element.177), channel_id=1, source_target_pairs={{0,16},{2,18},{4,20},{6,22},{8,24},{10,26},{12,28},{14,30},{16,0},... | collective-permute-start | bytes 442376 | tf_op jit(solution)/shard_map/ppermute | solution.py:42
  110.7 2.2 %shard_map.292 = (f32[576,768]{1,0:T(8,128)S(1)}, bf16[576,768]{1,0:T(8,128)(2,1)S(1)}, bf16[576,384]{1,0:T(8,128)(2,1)S(1)}, f32[8,768]{1,0:T(8,128)S(1)}) custom-call(s32[1,768]{1,0:T(1,128)S(1)} %add.53.order_ref, f32[8,768]{1,0:T(8,128)S(1)} %get-tuple-element.160.row_ref, bf16[576,768]{1,0:T(8,128)(2,1)S(1)} %get-tuple-element.170.own_ref, ...), custom_call_target="tpu_custom_call" | custom-call | bytes 1024 | tf_op jit(solution)/shard_map/pallas_call | solution.py:71
  112.9 6.4 %shard_map.293 = (bf16[576,384]{1,0:T(8,128)(2,1)S(1)}, bf16[576,768]{1,0:T(8,128)(2,1)S(1)}) custom-call(s32[1,4]{1,0:T(1,128)S(1)} %copy-done.11, bf16[576,1152]{1,0:T(8,128)(2,1)S(1)} %get-tuple-element.140.qkv_ref, f32[8,576]{1,0:T(8,128)S(1)} %get-tuple-element.141.lse_ref, bf16[576,384]{1,0:T(8,128)(2,1)S(1)} %get-tuple-element.188.refs_0_), custom_call_target="tpu_custom_call" | custom-call | flops 99999997952 | bytes 1024 | tf_op jit(solution)/shard_map/pallas_call | solution.py:71
  123.2 3.1 %collective-permute-start.46 = (bf16[48,1536]{1,0:T(8,128)(2,1)S(1)}, bf16[48,1536]{1,0:T(8,128)(2,1)S(1)}, u32[]{:S(2)}, u32[]{:S(2)}) collective-permute-start(bf16[48,1536]{1,0:T(8,128)(2,1)S(1)} %get-tuple-element.200), channel_id=1, source_target_pairs={{0,16},{2,18},{4,20},{6,22},{8,24},{10,26},{12,28},{14,30},{16,0},... | collective-permute-start | bytes 442376 | tf_op jit(solution)/shard_map/ppermute | solution.py:42
  129.5 1.8 %shard_map.297 = (bf16[576,768]{1,0:T(8,128)(2,1)S(1)}, f32[1,768]{1,0:T(1,128)S(1)}, f32[1,768]{1,0:T(1,128)S(1)}) custom-call(bf16[576,384]{1,0:T(8,128)(2,1)S(1)} %get-tuple-element.202.refs_3_.gq_ref, bf16[576,768]{1,0:T(8,128)(2,1)S(1)} %get-tuple-element.203.refs_5_.gkv_ref, bf16[576,768]{1,0:T(8,128)(2,1)S(1)} %get-tuple-element.146.ent_in.ent_ref, ...), custom_call_target="tpu_custom_call" | custom-call | flops 99999997952 | bytes 1024 | tf_op jit(solution)/shard_map/pallas_call | solution.py:71
  132.6 2.4 %collective-permute-done.40.gain_other = f32[1,768]{1,0:T(1,128)S(1)} collective-permute-done((f32[1,768]{1,0:T(1,128)S(1)}, f32[1,768]{1,0:T(1,128)S(1)}, u32[]{:S(2)}, u32[]{:S(2)}) %collective-permute-start.40) | collective-permute-done | bytes 3104 | tf_op jit(solution)/shard_map/ppermute | solution.py:47
  140.5 2.8 %collective-permute-done.42 = f32[48,128]{1,0:T(8,128)S(1)} collective-permute-done((f32[48,128]{1,0:T(8,128)S(1)}, f32[48,128]{1,0:T(8,128)S(1)}, u32[]{:S(2)}, u32[]{:S(2)}) %collective-permute-start.42) | collective-permute-done | bytes 24608 | tf_op jit(solution)/shard_map/ppermute | solution.py:42
  147.8 2.5 %shard_map.300 = bf16[576,767]{1,0:T(8,128)(2,1)} custom-call(s32[1,768]{1,0:T(1,128)S(1)} %add.53.order_ref, f32[8,768]{1,0:T(8,128)S(1)} %copy-done.3, f32[576,768]{1,0:T(8,128)S(1)} %get-tuple-element.186.mid_ref, bf16[576,768]{1,0:T(8,128)(2,1)S(1)} %shard_map.291.own_ref, bf16[576,768]{1,0:T(8,128)(2,1)S(1)} %collective-permute-done.36.other_ref), custom_call_target="tpu_custom_call" | custom-call | bytes 1024 | tf_op jit(solution)/shard_map/pallas_call | solution.py:71
  150.3 4.4 %collective-permute-done.39.other_ref = bf16[576,768]{1,0:T(8,128)(2,1)S(1)} collective-permute-done((bf16[576,768]{1,0:T(8,128)(2,1)S(1)}, bf16[576,768]{1,0:T(8,128)(2,1)S(1)}, u32[]{:S(2)}, u32[]{:S(2)}) %collective-permute-start.39) | collective-permute-done | bytes 884768 | tf_op jit(solution)/shard_map/ppermute | solution.py:47
  154.7 3.4 %shard_map.301 = bf16[576,767]{1,0:T(8,128)(2,1)} custom-call(s32[1,768]{1,0:T(1,128)S(1)} %add.53.order_ref, f32[8,768]{1,0:T(8,128)S(1)} %copy-done.3, bf16[576,768]{1,0:T(8,128)(2,1)S(1)} %get-tuple-element.204.own_ref, bf16[576,768]{1,0:T(8,128)(2,1)S(1)} %collective-permute-done.39.other_ref, bf16[576,768]{1,0:T(8,128)(2,1)S(1)} %get-tuple-element.146.ent_in.ent_ref, ...), custom_call_target="tpu_custom_call" | custom-call | bytes 1024 | tf_op jit(solution)/shard_map/pallas_call | solution.py:71
  158.1 3.3 %collective-permute-done.50.refs_2_ = bf16[48,1664]{1,0:T(8,128)(2,1)S(1)} collective-permute-done((bf16[48,1664]{1,0:T(8,128)(2,1)S(1)}, bf16[48,1664]{1,0:T(8,128)(2,1)S(1)}, u32[]{:S(2)}, u32[]{:S(2)}) %collective-permute-start.50) | collective-permute-done | bytes 159776 | tf_op jit(solution)/shard_map/ppermute | solution.py:42
  (155 shorter events, 61.4 us)
Async XLA Ops:
  2.2 15.3 %collective-permute-start.1 = (bf16[48,1152]{1,0:T(8,128)(2,1)}, bf16[48,1152]{1,0:T(8,128)(2,1)S(1)}, u32[]{:S(2)}, u32[]{:S(2)}) collective-permute-start(bf16[48,1152]{1,0:T(8,128)(2,1)} %shard_map.280), channel_id=1, source_target_pairs={{0,8},{2,10},{4,12},{6,14},{8,0},{10,2},{12,4},{14,6},{16,24},{18,... | collective-permute-start | bytes 331784 | tf_op jit(solution)/shard_map/ppermute | solution.py:42
  2.3 15.2 %collective-permute-start.2 = (bf16[48,1152]{1,0:T(8,128)(2,1)}, bf16[48,1152]{1,0:T(8,128)(2,1)S(1)}, u32[]{:S(2)}, u32[]{:S(2)}) collective-permute-start(bf16[48,1152]{1,0:T(8,128)(2,1)} %shard_map.280), channel_id=1, source_target_pairs={{0,16},{2,18},{4,20},{6,22},{8,24},{10,26},{12,28},{14,30},{16,0},... | collective-permute-start | bytes 331784 | tf_op jit(solution)/shard_map/ppermute | solution.py:42
  5.3 12.2 %collective-permute-start.3 = (bf16[48,1152]{1,0:T(8,128)(2,1)}, bf16[48,1152]{1,0:T(8,128)(2,1)S(1)}, u32[]{:S(2)}, u32[]{:S(2)}) collective-permute-start(bf16[48,1152]{1,0:T(8,128)(2,1)} %shard_map.280), channel_id=1, source_target_pairs={{0,24},{2,26},{4,28},{6,30},{8,16},{10,18},{12,20},{14,22},{16,8},... | collective-permute-start | bytes 331784 | tf_op jit(solution)/shard_map/ppermute | solution.py:42
  20.3 16.6 %collective-permute-start.12 = (bf16[48,2304]{1,0:T(8,128)(2,1)S(1)}, bf16[48,2304]{1,0:T(8,128)(2,1)S(1)}, u32[]{:S(2)}, u32[]{:S(2)}) collective-permute-start(bf16[48,2304]{1,0:T(8,128)(2,1)S(1)} %shard_map.281), channel_id=1, source_target_pairs={{0,8},{2,10},{4,12},{6,14},{8,0},{10,2},{12,4},{14,6},{16,24},{18,... | collective-permute-start | bytes 663560 | tf_op jit(solution)/shard_map/ppermute | solution.py:42
  24.9 15.8 %collective-permute-start.13 = (bf16[48,2304]{1,0:T(8,128)(2,1)S(1)}, bf16[48,2304]{1,0:T(8,128)(2,1)S(1)}, u32[]{:S(2)}, u32[]{:S(2)}) collective-permute-start(bf16[48,2304]{1,0:T(8,128)(2,1)S(1)} %shard_map.281), channel_id=1, source_target_pairs={{0,16},{2,18},{4,20},{6,22},{8,24},{10,26},{12,28},{14,30},{16,0},... | collective-permute-start | bytes 663560 | tf_op jit(solution)/shard_map/ppermute | solution.py:42
  28.4 15.6 %collective-permute-start.14 = (bf16[48,2304]{1,0:T(8,128)(2,1)S(1)}, bf16[48,2304]{1,0:T(8,128)(2,1)S(1)}, u32[]{:S(2)}, u32[]{:S(2)}) collective-permute-start(bf16[48,2304]{1,0:T(8,128)(2,1)S(1)} %shard_map.281), channel_id=1, source_target_pairs={{0,24},{2,26},{4,28},{6,30},{8,16},{10,18},{12,20},{14,22},{16,8},... | collective-permute-start | bytes 663560 | tf_op jit(solution)/shard_map/ppermute | solution.py:42
  44.1 27.2 %collective-permute-start.16 = (bf16[192,2304]{1,0:T(8,128)(2,1)S(1)}, bf16[192,2304]{1,0:T(8,128)(2,1)S(1)}, u32[]{:S(2)}, u32[]{:S(2)}) collective-permute-start(bf16[192,2304]{1,0:T(8,128)(2,1)S(1)} %constant_dynamic-update-slice_fusion.4.refs_0_), channel_id=1, source_target_pairs={{0,4},{2,6},{4,0},{6,2},{8,12},{10,14},{12,8},{14,10},{16,20},{18,... | collective-permute-start | bytes 2654216 | tf_op jit(solution)/shard_map/ppermute | solution.py:42
  46.3 20.4 %collective-permute-start.18 = (bf16[96,1536]{1,0:T(8,128)(2,1)S(1)}, bf16[96,1536]{1,0:T(8,128)(2,1)S(1)}, u32[]{:S(2)}, u32[]{:S(2)}) collective-permute-start(bf16[96,1536]{1,0:T(8,128)(2,1)S(1)} %maximum_maximum_fusion.refs_4_.refs_1_), channel_id=1, source_target_pairs={{0,16},{2,18},{4,20},{6,22},{8,24},{10,26},{12,28},{14,30},{16,0},... | collective-permute-start | bytes 884744 | tf_op jit(solution)/shard_map/ppermute | solution.py:42
  49.3 22.0 %collective-permute-start.19 = (bf16[96,1536]{1,0:T(8,128)(2,1)S(1)}, bf16[96,1536]{1,0:T(8,128)(2,1)S(1)}, u32[]{:S(2)}, u32[]{:S(2)}) collective-permute-start(bf16[96,1536]{1,0:T(8,128)(2,1)S(1)} %maximum_maximum_fusion.refs_4_.refs_1_), channel_id=1, source_target_pairs={{0,24},{2,26},{4,28},{6,30},{8,16},{10,18},{12,20},{14,22},{16,8},... | collective-permute-start | bytes 884744 | tf_op jit(solution)/shard_map/ppermute | solution.py:42
  85.9 23.5 %collective-permute-start.26 = (bf16[576,768]{1,0:T(8,128)(2,1)S(1)}, bf16[576,768]{1,0:T(8,128)(2,1)S(1)}, u32[]{:S(2)}, u32[]{:S(2)}) collective-permute-start(bf16[576,768]{1,0:T(8,128)(2,1)S(1)} %get-tuple-element.170.own_ref), channel_id=1, source_target_pairs={{0,1},{1,0},{2,3},{3,2},{4,5},{5,4},{6,7},{7,6},{8,9},{9,8},{10,11... | collective-permute-start | bytes 2654216 | tf_op jit(solution)/shard_map/ppermute | solution.py:47
  89.4 16.2 %collective-permute-start.29 = (bf16[192,1536]{1,0:T(8,128)(2,1)S(1)}, bf16[192,1536]{1,0:T(8,128)(2,1)S(1)}, u32[]{:S(2)}, u32[]{:S(2)}) collective-permute-start(bf16[192,1536]{1,0:T(8,128)(2,1)S(1)} %get-tuple-element.175), channel_id=1, source_target_pairs={{0,4},{2,6},{4,0},{6,2},{8,12},{10,14},{12,8},{14,10},{16,20},{18,... | collective-permute-start | bytes 1769480 | tf_op jit(solution)/shard_map/ppermute | solution.py:42
  92.0 27.2 %collective-permute-start.35 = (bf16[192,1536]{1,0:T(8,128)(2,1)S(1)}, bf16[192,1536]{1,0:T(8,128)(2,1)S(1)}, u32[]{:S(2)}, u32[]{:S(2)}) collective-permute-start(bf16[192,1536]{1,0:T(8,128)(2,1)S(1)} %get-tuple-element.183), channel_id=1, source_target_pairs={{0,4},{2,6},{4,0},{6,2},{8,12},{10,14},{12,8},{14,10},{16,20},{18,... | collective-permute-start | bytes 1769480 | tf_op jit(solution)/shard_map/ppermute | solution.py:42
  94.7 34.8 %collective-permute-start.36 = (bf16[576,768]{1,0:T(8,128)(2,1)S(1)}, bf16[576,768]{1,0:T(8,128)(2,1)S(1)}, u32[]{:S(2)}, u32[]{:S(2)}) collective-permute-start(bf16[576,768]{1,0:T(8,128)(2,1)S(1)} %shard_map.291.own_ref), channel_id=1, source_target_pairs={{0,1},{1,0},{2,3},{3,2},{4,5},{5,4},{6,7},{7,6},{8,9},{9,8},{10,11... | collective-permute-start | bytes 2654216 | tf_op jit(solution)/shard_map/ppermute | solution.py:47
  105.7 13.6 %collective-permute-start.32 = (bf16[48,1536]{1,0:T(8,128)(2,1)S(1)}, bf16[48,1536]{1,0:T(8,128)(2,1)S(1)}, u32[]{:S(2)}, u32[]{:S(2)}) collective-permute-start(bf16[48,1536]{1,0:T(8,128)(2,1)S(1)} %get-tuple-element.176), channel_id=1, source_target_pairs={{0,8},{2,10},{4,12},{6,14},{8,0},{10,2},{12,4},{14,6},{16,24},{18,... | collective-permute-start | bytes 442376 | tf_op jit(solution)/shard_map/ppermute | solution.py:42
  105.8 13.5 %collective-permute-start.33 = (bf16[48,1536]{1,0:T(8,128)(2,1)S(1)}, bf16[48,1536]{1,0:T(8,128)(2,1)S(1)}, u32[]{:S(2)}, u32[]{:S(2)}) collective-permute-start(bf16[48,1536]{1,0:T(8,128)(2,1)S(1)} %get-tuple-element.177), channel_id=1, source_target_pairs={{0,16},{2,18},{4,20},{6,22},{8,24},{10,26},{12,28},{14,30},{16,0},... | collective-permute-start | bytes 442376 | tf_op jit(solution)/shard_map/ppermute | solution.py:42
  109.5 11.6 %collective-permute-start.34 = (bf16[48,1536]{1,0:T(8,128)(2,1)S(1)}, bf16[48,1536]{1,0:T(8,128)(2,1)S(1)}, u32[]{:S(2)}, u32[]{:S(2)}) collective-permute-start(bf16[48,1536]{1,0:T(8,128)(2,1)S(1)} %get-tuple-element.178), channel_id=1, source_target_pairs={{0,24},{2,26},{4,28},{6,30},{8,16},{10,18},{12,20},{14,22},{16,8},... | collective-permute-start | bytes 442376 | tf_op jit(solution)/shard_map/ppermute | solution.py:42
  123.1 14.2 %collective-permute-start.45 = (bf16[48,1536]{1,0:T(8,128)(2,1)S(1)}, bf16[48,1536]{1,0:T(8,128)(2,1)S(1)}, u32[]{:S(2)}, u32[]{:S(2)}) collective-permute-start(bf16[48,1536]{1,0:T(8,128)(2,1)S(1)} %get-tuple-element.199), channel_id=1, source_target_pairs={{0,8},{2,10},{4,12},{6,14},{8,0},{10,2},{12,4},{14,6},{16,24},{18,... | collective-permute-start | bytes 442376 | tf_op jit(solution)/shard_map/ppermute | solution.py:42
  123.2 14.2 %collective-permute-start.46 = (bf16[48,1536]{1,0:T(8,128)(2,1)S(1)}, bf16[48,1536]{1,0:T(8,128)(2,1)S(1)}, u32[]{:S(2)}, u32[]{:S(2)}) collective-permute-start(bf16[48,1536]{1,0:T(8,128)(2,1)S(1)} %get-tuple-element.200), channel_id=1, source_target_pairs={{0,16},{2,18},{4,20},{6,22},{8,24},{10,26},{12,28},{14,30},{16,0},... | collective-permute-start | bytes 442376 | tf_op jit(solution)/shard_map/ppermute | solution.py:42
  126.3 13.4 %collective-permute-start.47 = (bf16[48,1536]{1,0:T(8,128)(2,1)S(1)}, bf16[48,1536]{1,0:T(8,128)(2,1)S(1)}, u32[]{:S(2)}, u32[]{:S(2)}) collective-permute-start(bf16[48,1536]{1,0:T(8,128)(2,1)S(1)} %get-tuple-element.201), channel_id=1, source_target_pairs={{0,24},{2,26},{4,28},{6,30},{8,16},{10,18},{12,20},{14,22},{16,8},... | collective-permute-start | bytes 442376 | tf_op jit(solution)/shard_map/ppermute | solution.py:42
  127.9 15.4 %collective-permute-start.44 = (bf16[192,1536]{1,0:T(8,128)(2,1)S(1)}, bf16[192,1536]{1,0:T(8,128)(2,1)S(1)}, u32[]{:S(2)}, u32[]{:S(2)}) collective-permute-start(bf16[192,1536]{1,0:T(8,128)(2,1)S(1)} %get-tuple-element.196), channel_id=1, source_target_pairs={{0,4},{2,6},{4,0},{6,2},{8,12},{10,14},{12,8},{14,10},{16,20},{18,... | collective-permute-start | bytes 1769480 | tf_op jit(solution)/shard_map/ppermute | solution.py:42
  135.0 19.7 %collective-permute-start.39 = (bf16[576,768]{1,0:T(8,128)(2,1)S(1)}, bf16[576,768]{1,0:T(8,128)(2,1)S(1)}, u32[]{:S(2)}, u32[]{:S(2)}) collective-permute-start(bf16[576,768]{1,0:T(8,128)(2,1)S(1)} %get-tuple-element.204.own_ref), channel_id=1, source_target_pairs={{0,1},{1,0},{2,3},{3,2},{4,5},{5,4},{6,7},{7,6},{8,9},{9,8},{10,11... | collective-permute-start | bytes 2654216 | tf_op jit(solution)/shard_map/ppermute | solution.py:47
  143.5 14.7 %collective-permute-start.48 = (bf16[48,1664]{1,0:T(8,128)(2,1)S(1)}, bf16[48,1664]{1,0:T(8,128)(2,1)S(1)}, u32[]{:S(2)}, u32[]{:S(2)}) collective-permute-start(bf16[48,1664]{1,0:T(8,128)(2,1)S(1)} %get-tuple-element.216), channel_id=1, source_target_pairs={{0,8},{2,10},{4,12},{6,14},{8,0},{10,2},{12,4},{14,6},{16,24},{18,... | collective-permute-start | bytes 479240 | tf_op jit(solution)/shard_map/ppermute | solution.py:42
  144.9 13.3 %collective-permute-start.49 = (bf16[48,1664]{1,0:T(8,128)(2,1)S(1)}, bf16[48,1664]{1,0:T(8,128)(2,1)S(1)}, u32[]{:S(2)}, u32[]{:S(2)}) collective-permute-start(bf16[48,1664]{1,0:T(8,128)(2,1)S(1)} %get-tuple-element.217), channel_id=1, source_target_pairs={{0,16},{2,18},{4,20},{6,22},{8,24},{10,26},{12,28},{14,30},{16,0},... | collective-permute-start | bytes 479240 | tf_op jit(solution)/shard_map/ppermute | solution.py:42
  146.6 14.8 %collective-permute-start.50 = (bf16[48,1664]{1,0:T(8,128)(2,1)S(1)}, bf16[48,1664]{1,0:T(8,128)(2,1)S(1)}, u32[]{:S(2)}, u32[]{:S(2)}) collective-permute-start(bf16[48,1664]{1,0:T(8,128)(2,1)S(1)} %get-tuple-element.218), channel_id=1, source_target_pairs={{0,24},{2,26},{4,28},{6,30},{8,16},{10,18},{12,20},{14,22},{16,8},... | collective-permute-start | bytes 479240 | tf_op jit(solution)/shard_map/ppermute | solution.py:42
  (43 other events, 403.9 us)

commit v3 on v1

--- a/solution.py
+++ b/solution.py
@@ -770,7 +770,6 @@
         [lengths, qkv, lse] + gctx,
         scalars=1,
         scratch=[pltpu.VMEM((rows, rows), F32), pltpu.VMEM((rows, PAIR), F32), pltpu.VMEM((rows, PAIR), F32)],
-        cost=LONG,
     )
     gq, gkv = tie([sum_dn, sum_up], gq, gkv)
     sum_last = Sum([(gba, (context,)), ((acts_a,), (gq,)), ((acts_a,), (gkv,))], count, first=2).go()

time: 163 us -> 163 us (level)
    unnamed x37 -> x33, local copies, waits for them, and re-layouts: 3.66 us -> 3.65 us
  transfers between devices with their start and end apart: 51 -> 51, of which waited for: 22 -> 23; matrix products, arithmetic and copies ran while one was open for 2% -> 2% of each run, Pallas kernels for 21% -> 21%
where the time goes in v3:
time: 163 us
  waiting for transfers between devices  61.8 us (38%)
  starting transfers between devices  47.2 us (29%)
  Pallas kernels  45.3 us (28%)
  local copies, waits for them, and re-layouts  4.73 us (3%)
  other arithmetic  2.33 us (1%)
    ppermute x45, waiting for transfers between devices, swap(): return lax.ppermute(array, 'dp', [(i, i ^ flip) for i in range(count)])  50.5 us
    pallas_call x21, Pallas kernels, call(): pl.pallas_call(kernel, out_shape=outs, in_specs=[SMEM] * scalars + [VMEM]...  43.7 us
    ppermute x45, starting transfers between devices, swap(): return lax.ppermute(array, 'dp', [(i, i ^ flip) for i in range(count)])  40.7 us
    ppermute x6, waiting for transfers between devices, swap_tensor(): return lax.ppermute(array, 'tensor', [(i, i ^ 1) for i in range(count)])  11.3 us
    ppermute x6, starting transfers between devices, swap_tensor(): return lax.ppermute(array, 'tensor', [(i, i ^ 1) for i in range(count)])  6.58 us
    unnamed x33, local copies, waits for them, and re-layouts  3.65 us
  transfers between devices with their start and end apart: 51, of which 23 were waited for; matrix products, arithmetic and copies ran while one was open for 2% of the time, Pallas kernels for 21%

profile of v3, /device:TPU:8, one launch (start us, length us, event | category | flops | bytes accessed | tf_op | source)
XLA Modules:
  0.0 162.6 jit_solution(3471257647792821018)
XLA Ops:
  2.3 3.0 %collective-permute-start.2 = (bf16[48,1152]{1,0:T(8,128)(2,1)}, bf16[48,1152]{1,0:T(8,128)(2,1)S(1)}, u32[]{:S(2)}, u32[]{:S(2)}) collective-permute-start(bf16[48,1152]{1,0:T(8,128)(2,1)} %shard_map.280), channel_id=1, source_target_pairs={{0,16},{2,18},{4,20},{6,22},{8,24},{10,26},{12,28},{14,30},{16,0},... | collective-permute-start | bytes 331784 | tf_op jit(solution)/shard_map/ppermute | solution.py:42
  22.0 3.2 %collective-permute-done.7.refs_3_ = bf16[96,1152]{1,0:T(8,128)(2,1)S(1)} collective-permute-done((bf16[96,1152]{1,0:T(8,128)(2,1)S(1)}, bf16[96,1152]{1,0:T(8,128)(2,1)S(1)}, u32[]{:S(2)}, u32[]{:S(2)}) %collective-permute-start.7) | collective-permute-done | bytes 221216 | tf_op jit(solution)/shard_map/ppermute | solution.py:42
  25.2 3.5 %collective-permute-start.13 = (bf16[48,2304]{1,0:T(8,128)(2,1)S(1)}, bf16[48,2304]{1,0:T(8,128)(2,1)S(1)}, u32[]{:S(2)}, u32[]{:S(2)}) collective-permute-start(bf16[48,2304]{1,0:T(8,128)(2,1)S(1)} %shard_map.281), channel_id=1, source_target_pairs={{0,16},{2,18},{4,20},{6,22},{8,24},{10,26},{12,28},{14,30},{16,0},... | collective-permute-start | bytes 663560 | tf_op jit(solution)/shard_map/ppermute | solution.py:42
  31.3 5.9 %shard_map.283 = (bf16[576,1152]{1,0:T(8,128)(2,1)S(1)}, bf16[576,384]{1,0:T(8,128)(2,1)S(1)}, f32[8,576]{1,0:T(8,128)S(1)}) custom-call(s32[1,4]{1,0:T(1,128)S(1)} %copy-done.9, bf16[576,768]{1,0:T(8,128)(2,1)S(1)} %get-tuple-element.135.acts_ref.refs_2_.refs_4_, f32[1,1152]{1,0:T(1,128)S(1)} %fusion.1.bias_ref, ...), custom_call_target="tpu_custom_call" | custom-call | bytes 1024 | tf_op jit(solution)/shard_map/pallas_call | solution.py:71
  37.2 3.8 %collective-permute-done.13 = bf16[48,2304]{1,0:T(8,128)(2,1)S(1)} collective-permute-done((bf16[48,2304]{1,0:T(8,128)(2,1)S(1)}, bf16[48,2304]{1,0:T(8,128)(2,1)S(1)}, u32[]{:S(2)}, u32[]{:S(2)}) %collective-permute-start.13) | collective-permute-done | bytes 221216 | tf_op jit(solution)/shard_map/ppermute | solution.py:42
  41.0 3.3 %collective-permute-done.14 = bf16[48,2304]{1,0:T(8,128)(2,1)S(1)} collective-permute-done((bf16[48,2304]{1,0:T(8,128)(2,1)S(1)}, bf16[48,2304]{1,0:T(8,128)(2,1)S(1)}, u32[]{:S(2)}, u32[]{:S(2)}) %collective-permute-start.14) | collective-permute-done | bytes 221216 | tf_op jit(solution)/shard_map/ppermute | solution.py:42
  46.7 3.0 %collective-permute-start.18 = (bf16[96,1536]{1,0:T(8,128)(2,1)S(1)}, bf16[96,1536]{1,0:T(8,128)(2,1)S(1)}, u32[]{:S(2)}, u32[]{:S(2)}) collective-permute-start(bf16[96,1536]{1,0:T(8,128)(2,1)S(1)} %maximum_maximum_fusion.refs_4_.refs_1_), channel_id=1, source_target_pairs={{0,16},{2,18},{4,20},{6,22},{8,24},{10,26},{12,28},{14,30},{16,0},... | collective-permute-start | bytes 884744 | tf_op jit(solution)/shard_map/ppermute | solution.py:42
  50.2 3.2 %collective-permute-done.15.other_ref = bf16[576,384]{1,0:T(8,128)(2,1)S(1)} collective-permute-done((bf16[576,384]{1,0:T(8,128)(2,1)S(1)}, bf16[576,384]{1,0:T(8,128)(2,1)S(1)}, u32[]{:S(2)}, u32[]{:S(2)}) %collective-permute-start.15) | collective-permute-done | bytes 442400 | tf_op jit(solution)/shard_map/ppermute | solution.py:47
  56.6 10.5 %collective-permute-done.18.refs_6_.refs_3_ = bf16[96,1536]{1,0:T(8,128)(2,1)S(1)} collective-permute-done((bf16[96,1536]{1,0:T(8,128)(2,1)S(1)}, bf16[96,1536]{1,0:T(8,128)(2,1)S(1)}, u32[]{:S(2)}, u32[]{:S(2)}) %collective-permute-start.18) | collective-permute-done | bytes 294944 | tf_op jit(solution)/shard_map/ppermute | solution.py:42
  67.1 4.5 %collective-permute-done.19.refs_7_.refs_4_ = bf16[96,1536]{1,0:T(8,128)(2,1)S(1)} collective-permute-done((bf16[96,1536]{1,0:T(8,128)(2,1)S(1)}, bf16[96,1536]{1,0:T(8,128)(2,1)S(1)}, u32[]{:S(2)}, u32[]{:S(2)}) %collective-permute-start.19) | collective-permute-done | bytes 294944 | tf_op jit(solution)/shard_map/ppermute | solution.py:42
  72.7 3.1 %collective-permute-done.22.refs_8_.refs_5_ = bf16[96,1536]{1,0:T(8,128)(2,1)S(1)} collective-permute-done((bf16[96,1536]{1,0:T(8,128)(2,1)S(1)}, bf16[96,1536]{1,0:T(8,128)(2,1)S(1)}, u32[]{:S(2)}, u32[]{:S(2)}) %collective-permute-start.22) | collective-permute-done | bytes 294944 | tf_op jit(solution)/shard_map/ppermute | solution.py:42
  77.4 7.3 %shard_map.285 = (f32[576,768]{1,0:T(8,128)S(1)}, bf16[576,768]{1,0:T(8,128)(2,1)S(1)}, bf16[576,1536]{1,0:T(8,128)(2,1)S(1)}, bf16[576,1536]{1,0:T(8,128)(2,1)S...) custom-call(s32[1,1]{1,0:T(1,128)} %bitcast.2.rank_ref, s32[1,768]{1,0:T(1,128)S(1)} %add.53.order_ref, ...), custom_call_target="tpu_custom_call" | custom-call | bytes 1024 | tf_op jit(solution)/shard_map/pallas_call | solution.py:71
  96.0 9.9 %collective-permute-done.29.refs_1_ = bf16[192,1536]{1,0:T(8,128)(2,1)S(1)} collective-permute-done((bf16[192,1536]{1,0:T(8,128)(2,1)S(1)}, bf16[192,1536]{1,0:T(8,128)(2,1)S(1)}, u32[]{:S(2)}, u32[]{:S(2)}) %collective-permute-start.29) | collective-permute-done | bytes 589856 | tf_op jit(solution)/shard_map/ppermute | solution.py:42
  106.2 3.7 %collective-permute-start.33 = (bf16[48,1536]{1,0:T(8,128)(2,1)S(1)}, bf16[48,1536]{1,0:T(8,128)(2,1)S(1)}, u32[]{:S(2)}, u32[]{:S(2)}) collective-permute-start(bf16[48,1536]{1,0:T(8,128)(2,1)S(1)} %get-tuple-element.177), channel_id=1, source_target_pairs={{0,16},{2,18},{4,20},{6,22},{8,24},{10,26},{12,28},{14,30},{16,0},... | collective-permute-start | bytes 442376 | tf_op jit(solution)/shard_map/ppermute | solution.py:42
  110.5 2.2 %collective-permute-start.34 = (bf16[48,1536]{1,0:T(8,128)(2,1)S(1)}, bf16[48,1536]{1,0:T(8,128)(2,1)S(1)}, u32[]{:S(2)}, u32[]{:S(2)}) collective-permute-start(bf16[48,1536]{1,0:T(8,128)(2,1)S(1)} %get-tuple-element.178), channel_id=1, source_target_pairs={{0,24},{2,26},{4,28},{6,30},{8,16},{10,18},{12,20},{14,22},{16,8},... | collective-permute-start | bytes 442376 | tf_op jit(solution)/shard_map/ppermute | solution.py:42
  112.7 2.7 %shard_map.292 = (f32[576,768]{1,0:T(8,128)S(1)}, bf16[576,768]{1,0:T(8,128)(2,1)S(1)}, bf16[576,384]{1,0:T(8,128)(2,1)S(1)}, f32[8,768]{1,0:T(8,128)S(1)}) custom-call(s32[1,768]{1,0:T(1,128)S(1)} %add.53.order_ref, f32[8,768]{1,0:T(8,128)S(1)} %get-tuple-element.160.row_ref, bf16[576,768]{1,0:T(8,128)(2,1)S(1)} %get-tuple-element.170.own_ref, ...), custom_call_target="tpu_custom_call" | custom-call | bytes 1024 | tf_op jit(solution)/shard_map/pallas_call | solution.py:71
  115.4 6.1 %shard_map.293 = (bf16[576,384]{1,0:T(8,128)(2,1)S(1)}, bf16[576,768]{1,0:T(8,128)(2,1)S(1)}) custom-call(s32[1,4]{1,0:T(1,128)S(1)} %copy-done.9, bf16[576,1152]{1,0:T(8,128)(2,1)S(1)} %get-tuple-element.140.qkv_ref, f32[8,576]{1,0:T(8,128)S(1)} %get-tuple-element.141.lse_ref, bf16[576,384]{1,0:T(8,128)(2,1)S(1)} %get-tuple-element.188.refs_0_), custom_call_target="tpu_custom_call" | custom-call | bytes 1024 | tf_op jit(solution)/shard_map/pallas_call | solution.py:71
  123.6 2.9 %collective-permute-start.46 = (bf16[48,1536]{1,0:T(8,128)(2,1)S(1)}, bf16[48,1536]{1,0:T(8,128)(2,1)S(1)}, u32[]{:S(2)}, u32[]{:S(2)}) collective-permute-start(bf16[48,1536]{1,0:T(8,128)(2,1)S(1)} %get-tuple-element.200), channel_id=1, source_target_pairs={{0,16},{2,18},{4,20},{6,22},{8,24},{10,26},{12,28},{14,30},{16,0},... | collective-permute-start | bytes 442376 | tf_op jit(solution)/shard_map/ppermute | solution.py:42
  132.5 2.9 %collective-permute-done.40.gain_other = f32[1,768]{1,0:T(1,128)S(1)} collective-permute-done((f32[1,768]{1,0:T(1,128)S(1)}, f32[1,768]{1,0:T(1,128)S(1)}, u32[]{:S(2)}, u32[]{:S(2)}) %collective-permute-start.40) | collective-permute-done | bytes 3104 | tf_op jit(solution)/shard_map/ppermute | solution.py:47
  141.0 2.7 %collective-permute-done.42 = f32[48,128]{1,0:T(8,128)S(1)} collective-permute-done((f32[48,128]{1,0:T(8,128)S(1)}, f32[48,128]{1,0:T(8,128)S(1)}, u32[]{:S(2)}, u32[]{:S(2)}) %collective-permute-start.42) | collective-permute-done | bytes 24608 | tf_op jit(solution)/shard_map/ppermute | solution.py:42
  148.2 2.4 %shard_map.300 = bf16[576,767]{1,0:T(8,128)(2,1)} custom-call(s32[1,768]{1,0:T(1,128)S(1)} %add.53.order_ref, f32[8,768]{1,0:T(8,128)S(1)} %get-tuple-element.160.row_ref, f32[576,768]{1,0:T(8,128)S(1)} %get-tuple-element.186.mid_ref, bf16[576,768]{1,0:T(8,128)(2,1)S(1)} %shard_map.291.own_ref, bf16[576,768]{1,0:T(8,128)(2,1)S(1)} %collective-permute-done.36.other_ref), custom_call_target="tpu_custom_call" | custom-call | bytes 1024 | tf_op jit(solution)/shard_map/pallas_call | solution.py:71
  150.6 4.5 %collective-permute-done.39.other_ref = bf16[576,768]{1,0:T(8,128)(2,1)S(1)} collective-permute-done((bf16[576,768]{1,0:T(8,128)(2,1)S(1)}, bf16[576,768]{1,0:T(8,128)(2,1)S(1)}, u32[]{:S(2)}, u32[]{:S(2)}) %collective-permute-start.39) | collective-permute-done | bytes 884768 | tf_op jit(solution)/shard_map/ppermute | solution.py:47
  155.1 3.5 %shard_map.301 = bf16[576,767]{1,0:T(8,128)(2,1)} custom-call(s32[1,768]{1,0:T(1,128)S(1)} %add.53.order_ref, f32[8,768]{1,0:T(8,128)S(1)} %get-tuple-element.160.row_ref, bf16[576,768]{1,0:T(8,128)(2,1)S(1)} %get-tuple-element.204.own_ref, bf16[576,768]{1,0:T(8,128)(2,1)S(1)} %collective-permute-done.39.other_ref, ...), custom_call_target="tpu_custom_call" | custom-call | bytes 1024 | tf_op jit(solution)/shard_map/pallas_call | solution.py:71
  158.6 3.3 %collective-permute-done.50.refs_2_ = bf16[48,1664]{1,0:T(8,128)(2,1)S(1)} collective-permute-done((bf16[48,1664]{1,0:T(8,128)(2,1)S(1)}, bf16[48,1664]{1,0:T(8,128)(2,1)S(1)}, u32[]{:S(2)}, u32[]{:S(2)}) %collective-permute-start.50) | collective-permute-done | bytes 159776 | tf_op jit(solution)/shard_map/ppermute | solution.py:42
  (151 shorter events, 60.4 us)
Async XLA Ops:
  2.2 15.6 %collective-permute-start.1 = (bf16[48,1152]{1,0:T(8,128)(2,1)}, bf16[48,1152]{1,0:T(8,128)(2,1)S(1)}, u32[]{:S(2)}, u32[]{:S(2)}) collective-permute-start(bf16[48,1152]{1,0:T(8,128)(2,1)} %shard_map.280), channel_id=1, source_target_pairs={{0,8},{2,10},{4,12},{6,14},{8,0},{10,2},{12,4},{14,6},{16,24},{18,... | collective-permute-start | bytes 331784 | tf_op jit(solution)/shard_map/ppermute | solution.py:42
  2.3 15.6 %collective-permute-start.2 = (bf16[48,1152]{1,0:T(8,128)(2,1)}, bf16[48,1152]{1,0:T(8,128)(2,1)S(1)}, u32[]{:S(2)}, u32[]{:S(2)}) collective-permute-start(bf16[48,1152]{1,0:T(8,128)(2,1)} %shard_map.280), channel_id=1, source_target_pairs={{0,16},{2,18},{4,20},{6,22},{8,24},{10,26},{12,28},{14,30},{16,0},... | collective-permute-start | bytes 331784 | tf_op jit(solution)/shard_map/ppermute | solution.py:42
  5.3 12.5 %collective-permute-start.3 = (bf16[48,1152]{1,0:T(8,128)(2,1)}, bf16[48,1152]{1,0:T(8,128)(2,1)S(1)}, u32[]{:S(2)}, u32[]{:S(2)}) collective-permute-start(bf16[48,1152]{1,0:T(8,128)(2,1)} %shard_map.280), channel_id=1, source_target_pairs={{0,24},{2,26},{4,28},{6,30},{8,16},{10,18},{12,20},{14,22},{16,8},... | collective-permute-start | bytes 331784 | tf_op jit(solution)/shard_map/ppermute | solution.py:42
  20.6 16.6 %collective-permute-start.12 = (bf16[48,2304]{1,0:T(8,128)(2,1)S(1)}, bf16[48,2304]{1,0:T(8,128)(2,1)S(1)}, u32[]{:S(2)}, u32[]{:S(2)}) collective-permute-start(bf16[48,2304]{1,0:T(8,128)(2,1)S(1)} %shard_map.281), channel_id=1, source_target_pairs={{0,8},{2,10},{4,12},{6,14},{8,0},{10,2},{12,4},{14,6},{16,24},{18,... | collective-permute-start | bytes 663560 | tf_op jit(solution)/shard_map/ppermute | solution.py:42
  25.2 15.8 %collective-permute-start.13 = (bf16[48,2304]{1,0:T(8,128)(2,1)S(1)}, bf16[48,2304]{1,0:T(8,128)(2,1)S(1)}, u32[]{:S(2)}, u32[]{:S(2)}) collective-permute-start(bf16[48,2304]{1,0:T(8,128)(2,1)S(1)} %shard_map.281), channel_id=1, source_target_pairs={{0,16},{2,18},{4,20},{6,22},{8,24},{10,26},{12,28},{14,30},{16,0},... | collective-permute-start | bytes 663560 | tf_op jit(solution)/shard_map/ppermute | solution.py:42
  28.7 15.6 %collective-permute-start.14 = (bf16[48,2304]{1,0:T(8,128)(2,1)S(1)}, bf16[48,2304]{1,0:T(8,128)(2,1)S(1)}, u32[]{:S(2)}, u32[]{:S(2)}) collective-permute-start(bf16[48,2304]{1,0:T(8,128)(2,1)S(1)} %shard_map.281), channel_id=1, source_target_pairs={{0,24},{2,26},{4,28},{6,30},{8,16},{10,18},{12,20},{14,22},{16,8},... | collective-permute-start | bytes 663560 | tf_op jit(solution)/shard_map/ppermute | solution.py:42
  44.5 27.2 %collective-permute-start.16 = (bf16[192,2304]{1,0:T(8,128)(2,1)S(1)}, bf16[192,2304]{1,0:T(8,128)(2,1)S(1)}, u32[]{:S(2)}, u32[]{:S(2)}) collective-permute-start(bf16[192,2304]{1,0:T(8,128)(2,1)S(1)} %constant_dynamic-update-slice_fusion.4.refs_0_), channel_id=1, source_target_pairs={{0,4},{2,6},{4,0},{6,2},{8,12},{10,14},{12,8},{14,10},{16,20},{18,... | collective-permute-start | bytes 2654216 | tf_op jit(solution)/shard_map/ppermute | solution.py:42
  46.7 20.5 %collective-permute-start.18 = (bf16[96,1536]{1,0:T(8,128)(2,1)S(1)}, bf16[96,1536]{1,0:T(8,128)(2,1)S(1)}, u32[]{:S(2)}, u32[]{:S(2)}) collective-permute-start(bf16[96,1536]{1,0:T(8,128)(2,1)S(1)} %maximum_maximum_fusion.refs_4_.refs_1_), channel_id=1, source_target_pairs={{0,16},{2,18},{4,20},{6,22},{8,24},{10,26},{12,28},{14,30},{16,0},... | collective-permute-start | bytes 884744 | tf_op jit(solution)/shard_map/ppermute | solution.py:42
  49.7 22.0 %collective-permute-start.19 = (bf16[96,1536]{1,0:T(8,128)(2,1)S(1)}, bf16[96,1536]{1,0:T(8,128)(2,1)S(1)}, u32[]{:S(2)}, u32[]{:S(2)}) collective-permute-start(bf16[96,1536]{1,0:T(8,128)(2,1)S(1)} %maximum_maximum_fusion.refs_4_.refs_1_), channel_id=1, source_target_pairs={{0,24},{2,26},{4,28},{6,30},{8,16},{10,18},{12,20},{14,22},{16,8},... | collective-permute-start | bytes 884744 | tf_op jit(solution)/shard_map/ppermute | solution.py:42
  88.0 22.5 %collective-permute-start.26 = (bf16[576,768]{1,0:T(8,128)(2,1)S(1)}, bf16[576,768]{1,0:T(8,128)(2,1)S(1)}, u32[]{:S(2)}, u32[]{:S(2)}) collective-permute-start(bf16[576,768]{1,0:T(8,128)(2,1)S(1)} %get-tuple-element.170.own_ref), channel_id=1, source_target_pairs={{0,1},{1,0},{2,3},{3,2},{4,5},{5,4},{6,7},{7,6},{8,9},{9,8},{10,11... | collective-permute-start | bytes 2654216 | tf_op jit(solution)/shard_map/ppermute | solution.py:47
  89.7 16.2 %collective-permute-start.29 = (bf16[192,1536]{1,0:T(8,128)(2,1)S(1)}, bf16[192,1536]{1,0:T(8,128)(2,1)S(1)}, u32[]{:S(2)}, u32[]{:S(2)}) collective-permute-start(bf16[192,1536]{1,0:T(8,128)(2,1)S(1)} %get-tuple-element.175), channel_id=1, source_target_pairs={{0,4},{2,6},{4,0},{6,2},{8,12},{10,14},{12,8},{14,10},{16,20},{18,... | collective-permute-start | bytes 1769480 | tf_op jit(solution)/shard_map/ppermute | solution.py:42
  92.4 29.2 %collective-permute-start.35 = (bf16[192,1536]{1,0:T(8,128)(2,1)S(1)}, bf16[192,1536]{1,0:T(8,128)(2,1)S(1)}, u32[]{:S(2)}, u32[]{:S(2)}) collective-permute-start(bf16[192,1536]{1,0:T(8,128)(2,1)S(1)} %get-tuple-element.183), channel_id=1, source_target_pairs={{0,4},{2,6},{4,0},{6,2},{8,12},{10,14},{12,8},{14,10},{16,20},{18,... | collective-permute-start | bytes 1769480 | tf_op jit(solution)/shard_map/ppermute | solution.py:42
  94.6 35.3 %collective-permute-start.36 = (bf16[576,768]{1,0:T(8,128)(2,1)S(1)}, bf16[576,768]{1,0:T(8,128)(2,1)S(1)}, u32[]{:S(2)}, u32[]{:S(2)}) collective-permute-start(bf16[576,768]{1,0:T(8,128)(2,1)S(1)} %shard_map.291.own_ref), channel_id=1, source_target_pairs={{0,1},{1,0},{2,3},{3,2},{4,5},{5,4},{6,7},{7,6},{8,9},{9,8},{10,11... | collective-permute-start | bytes 2654216 | tf_op jit(solution)/shard_map/ppermute | solution.py:47
  106.1 15.5 %collective-permute-start.32 = (bf16[48,1536]{1,0:T(8,128)(2,1)S(1)}, bf16[48,1536]{1,0:T(8,128)(2,1)S(1)}, u32[]{:S(2)}, u32[]{:S(2)}) collective-permute-start(bf16[48,1536]{1,0:T(8,128)(2,1)S(1)} %get-tuple-element.176), channel_id=1, source_target_pairs={{0,8},{2,10},{4,12},{6,14},{8,0},{10,2},{12,4},{14,6},{16,24},{18,... | collective-permute-start | bytes 442376 | tf_op jit(solution)/shard_map/ppermute | solution.py:42
  106.2 15.4 %collective-permute-start.33 = (bf16[48,1536]{1,0:T(8,128)(2,1)S(1)}, bf16[48,1536]{1,0:T(8,128)(2,1)S(1)}, u32[]{:S(2)}, u32[]{:S(2)}) collective-permute-start(bf16[48,1536]{1,0:T(8,128)(2,1)S(1)} %get-tuple-element.177), channel_id=1, source_target_pairs={{0,16},{2,18},{4,20},{6,22},{8,24},{10,26},{12,28},{14,30},{16,0},... | collective-permute-start | bytes 442376 | tf_op jit(solution)/shard_map/ppermute | solution.py:42
  110.5 11.1 %collective-permute-start.34 = (bf16[48,1536]{1,0:T(8,128)(2,1)S(1)}, bf16[48,1536]{1,0:T(8,128)(2,1)S(1)}, u32[]{:S(2)}, u32[]{:S(2)}) collective-permute-start(bf16[48,1536]{1,0:T(8,128)(2,1)S(1)} %get-tuple-element.178), channel_id=1, source_target_pairs={{0,24},{2,26},{4,28},{6,30},{8,16},{10,18},{12,20},{14,22},{16,8},... | collective-permute-start | bytes 442376 | tf_op jit(solution)/shard_map/ppermute | solution.py:42
  123.5 13.6 %collective-permute-start.45 = (bf16[48,1536]{1,0:T(8,128)(2,1)S(1)}, bf16[48,1536]{1,0:T(8,128)(2,1)S(1)}, u32[]{:S(2)}, u32[]{:S(2)}) collective-permute-start(bf16[48,1536]{1,0:T(8,128)(2,1)S(1)} %get-tuple-element.199), channel_id=1, source_target_pairs={{0,8},{2,10},{4,12},{6,14},{8,0},{10,2},{12,4},{14,6},{16,24},{18,... | collective-permute-start | bytes 442376 | tf_op jit(solution)/shard_map/ppermute | solution.py:42
  123.6 13.7 %collective-permute-start.46 = (bf16[48,1536]{1,0:T(8,128)(2,1)S(1)}, bf16[48,1536]{1,0:T(8,128)(2,1)S(1)}, u32[]{:S(2)}, u32[]{:S(2)}) collective-permute-start(bf16[48,1536]{1,0:T(8,128)(2,1)S(1)} %get-tuple-element.200), channel_id=1, source_target_pairs={{0,16},{2,18},{4,20},{6,22},{8,24},{10,26},{12,28},{14,30},{16,0},... | collective-permute-start | bytes 442376 | tf_op jit(solution)/shard_map/ppermute | solution.py:42
  126.6 13.6 %collective-permute-start.47 = (bf16[48,1536]{1,0:T(8,128)(2,1)S(1)}, bf16[48,1536]{1,0:T(8,128)(2,1)S(1)}, u32[]{:S(2)}, u32[]{:S(2)}) collective-permute-start(bf16[48,1536]{1,0:T(8,128)(2,1)S(1)} %get-tuple-element.201), channel_id=1, source_target_pairs={{0,24},{2,26},{4,28},{6,30},{8,16},{10,18},{12,20},{14,22},{16,8},... | collective-permute-start | bytes 442376 | tf_op jit(solution)/shard_map/ppermute | solution.py:42
  128.4 15.4 %collective-permute-start.44 = (bf16[192,1536]{1,0:T(8,128)(2,1)S(1)}, bf16[192,1536]{1,0:T(8,128)(2,1)S(1)}, u32[]{:S(2)}, u32[]{:S(2)}) collective-permute-start(bf16[192,1536]{1,0:T(8,128)(2,1)S(1)} %get-tuple-element.196), channel_id=1, source_target_pairs={{0,4},{2,6},{4,0},{6,2},{8,12},{10,14},{12,8},{14,10},{16,20},{18,... | collective-permute-start | bytes 1769480 | tf_op jit(solution)/shard_map/ppermute | solution.py:42
  135.4 19.7 %collective-permute-start.39 = (bf16[576,768]{1,0:T(8,128)(2,1)S(1)}, bf16[576,768]{1,0:T(8,128)(2,1)S(1)}, u32[]{:S(2)}, u32[]{:S(2)}) collective-permute-start(bf16[576,768]{1,0:T(8,128)(2,1)S(1)} %get-tuple-element.204.own_ref), channel_id=1, source_target_pairs={{0,1},{1,0},{2,3},{3,2},{4,5},{5,4},{6,7},{7,6},{8,9},{9,8},{10,11... | collective-permute-start | bytes 2654216 | tf_op jit(solution)/shard_map/ppermute | solution.py:47
  143.9 14.7 %collective-permute-start.48 = (bf16[48,1664]{1,0:T(8,128)(2,1)S(1)}, bf16[48,1664]{1,0:T(8,128)(2,1)S(1)}, u32[]{:S(2)}, u32[]{:S(2)}) collective-permute-start(bf16[48,1664]{1,0:T(8,128)(2,1)S(1)} %get-tuple-element.216), channel_id=1, source_target_pairs={{0,8},{2,10},{4,12},{6,14},{8,0},{10,2},{12,4},{14,6},{16,24},{18,... | collective-permute-start | bytes 479240 | tf_op jit(solution)/shard_map/ppermute | solution.py:42
  145.2 13.4 %collective-permute-start.49 = (bf16[48,1664]{1,0:T(8,128)(2,1)S(1)}, bf16[48,1664]{1,0:T(8,128)(2,1)S(1)}, u32[]{:S(2)}, u32[]{:S(2)}) collective-permute-start(bf16[48,1664]{1,0:T(8,128)(2,1)S(1)} %get-tuple-element.217), channel_id=1, source_target_pairs={{0,16},{2,18},{4,20},{6,22},{8,24},{10,26},{12,28},{14,30},{16,0},... | collective-permute-start | bytes 479240 | tf_op jit(solution)/shard_map/ppermute | solution.py:42
  146.9 14.9 %collective-permute-start.50 = (bf16[48,1664]{1,0:T(8,128)(2,1)S(1)}, bf16[48,1664]{1,0:T(8,128)(2,1)S(1)}, u32[]{:S(2)}, u32[]{:S(2)}) collective-permute-start(bf16[48,1664]{1,0:T(8,128)(2,1)S(1)} %get-tuple-element.218), channel_id=1, source_target_pairs={{0,24},{2,26},{4,28},{6,30},{8,16},{10,18},{12,20},{14,22},{16,8},... | collective-permute-start | bytes 479240 | tf_op jit(solution)/shard_map/ppermute | solution.py:42
  (41 other events, 343.4 us)
